TPU v7x, 32 devices: a whole 2x2x4 slice. The times are simulated.
32 devices in a mesh: grp: 4 (over x, core), seq: 8 (over z, y).
Axes of the slice: x: 2, y: 2, z: 4, core: 2. Of those that a mesh axis runs over, the one named last changes fastest.
Arguments:
- fields: bfloat16 [4096, 192], P(('grp', 'seq')), may hold values from -6 to 6
- patch_weight: bfloat16 [192, 1024], P(None, ('grp', 'seq')), may hold values from -3 to 3
- variable_embed: bfloat16 [48, 1024], P(None, ('grp', 'seq')), may hold values from -6 to 6
- query_vector: bfloat16 [1024], P(('grp', 'seq')), may hold values from -6 to 6
- key_weight: bfloat16 [1024, 1024], P(('grp', 'seq')), may hold values from -0.1875 to 0.1875
- value_weight: bfloat16 [1024, 1024], P(('grp', 'seq')), may hold values from -0.1875 to 0.1875
- merge_weight: bfloat16 [1024, 1024], P(('grp', 'seq')), may hold values from -0.75 to 0.75
- merge_bias: bfloat16 [1024], P(('grp', 'seq')), may hold values from -3 to 3
- position_table: bfloat16 [1024, 1024], P('seq', 'grp'), may hold values from -3 to 3
- lead_weight: bfloat16 [1024], P(('grp', 'seq')), may hold values from -6 to 6
- lead_bias: bfloat16 [1024], P(('grp', 'seq')), may hold values from -3 to 3
- first_gain: bfloat16 [1024], P(('grp', 'seq')), may hold values from 0.25 to 1.75
- first_shift: bfloat16 [1024], P(('grp', 'seq')), may hold values from -3 to 3
- joint_weight: bfloat16 [1024, 3072], P(('grp', 'seq')), may hold values from -0.1875 to 0.1875
- joint_bias: bfloat16 [2, 1024], P(None, ('grp', 'seq')), may hold values from -3 to 3
- output_weight: bfloat16 [1024, 1024], P(('grp', 'seq')), may hold values from -6 to 6
- output_bias: bfloat16 [1024], P(('grp', 'seq')), may hold values from -8 to 8
- second_gain: bfloat16 [1024], P(('grp', 'seq')), may hold values from 0.25 to 1.75
- second_shift: bfloat16 [1024], P(('grp', 'seq')), may hold values from -3 to 3
- expand_weight: bfloat16 [1024, 4096], P(('grp', 'seq')), may hold values from -0.1875 to 0.1875
- expand_bias: bfloat16 [4096], P(('grp', 'seq')), may hold values from -3 to 3
- reduce_weight: bfloat16 [4096, 1024], P(('grp', 'seq')), may hold values from -0.09375 to 0.09375
- reduce_bias: bfloat16 [1024], P(('grp', 'seq')), may hold values from -12 to 12
- segment_ids: int32 [4096], P(('grp', 'seq')), may hold values from 0 to 3, as said below
- live_rows: int32 [4096], P(('grp', 'seq')), may hold values from 0 to 1
- lead_steps: int32 [4, 4], P('grp'), may hold values from 1 to 28
- cotangent: bfloat16 [4096, 1024], P(('grp', 'seq')), may hold values from -6 to 6
Outputs:
- activations: float32 [4096, 1024], P(('grp', 'seq'))
- field_grad: float32 [4096, 192], P(('grp', 'seq'))
- grad_patch_weight: float32 [192, 1024], P(None, ('grp', 'seq'))
- grad_variable_embed: float32 [48, 1024], P(None, ('grp', 'seq'))
- grad_query_vector: float32 [1024], P(('grp', 'seq'))
- grad_key_weight: float32 [1024, 1024], P(('grp', 'seq'))
- grad_value_weight: float32 [1024, 1024], P(('grp', 'seq'))
- grad_merge_weight: float32 [1024, 1024], P(('grp', 'seq'))
- grad_merge_bias: float32 [1024], P(('grp', 'seq'))
- grad_position_table: float32 [1024, 1024], P('seq', 'grp')
- grad_lead_weight: float32 [1024], P(('grp', 'seq'))
- grad_lead_bias: float32 [1024], P(('grp', 'seq'))
- grad_first_gain: float32 [1024], P(('grp', 'seq'))
- grad_first_shift: float32 [1024], P(('grp', 'seq'))
- grad_joint_weight: float32 [1024, 3072], P(('grp', 'seq'))
- grad_joint_bias: float32 [2, 1024], P(None, ('grp', 'seq'))
- grad_output_weight: float32 [1024, 1024], P(('grp', 'seq'))
- grad_output_bias: float32 [1024], P(('grp', 'seq'))
- grad_second_gain: float32 [1024], P(('grp', 'seq'))
- grad_second_shift: float32 [1024], P(('grp', 'seq'))
- grad_expand_weight: float32 [1024, 4096], P(('grp', 'seq'))
- grad_expand_bias: float32 [4096], P(('grp', 'seq'))
- grad_reduce_weight: float32 [4096, 1024], P(('grp', 'seq'))
- grad_reduce_bias: float32 [1024], P(('grp', 'seq'))
Inputs may be any that keep to these rules, and one draw needn't show every extreme that they name: `segment_ids`: ids are compared only within a group of 1024 rows; in every group each id that occurs has rows with live_rows equal to 1.
All inputs are finite; a program needn't handle non-finite values.
Results may differ from a plain program's by a relative error of at most 0.023.
Values may be sent and summed in bfloat16 or wider, within the bound.
A program may use at most 384 MiB of HBM per device.

v0:
```python
import types

import jax
import jax.numpy as jnp
from jax import lax
from jax.experimental import pallas as pl
from jax.experimental.pallas import tpu as pltpu
from jax.sharding import PartitionSpec as P

D = 1024
HEADS = 16
FF = 4096
VARS = 48
PIX = 4
HDIM = 64
VP = 192
KP = 256

EPSILON = 1e-05
SCALE = 0.125
LEAD_UNIT = 0.06
MASKED = -1e30

MESH = pl.DeviceIdType.MESH
ROWS = ("grp", "seq")
F32 = jnp.float32
BF16 = jnp.bfloat16


def f32(x):
    return x.astype(F32)


def low(x):
    return x.astype(BF16)


def dot(a, b, ca, cb):
    return lax.dot_general(a, b, (((ca,), (cb,)), ((), ())), preferred_element_type=F32)


def low_sums(x):
    return dot(jnp.ones((8, x.shape[0]), BF16), x, 1, 0)[0]


def exchange(axis, parts):
    return [
        lax.all_gather(a, axis, axis=0, tiled=False)
        if mode == "all"
        else lax.all_to_all(a, axis, 0, 0, tiled=False)
        for a, mode in parts
    ]


def norm_parts(x):
    center = x - jnp.mean(x, axis=-1, keepdims=True)
    spread = jnp.mean(center * center, axis=-1, keepdims=True)
    inverse = lax.rsqrt(spread + EPSILON)
    return center * inverse, inverse


def norm_back(hat, inverse, gain, grad):
    f = grad * gain
    return inverse * (
        f
        - jnp.mean(f, axis=-1, keepdims=True)
        - hat * jnp.mean(f * hat, axis=-1, keepdims=True)
    )


def pack(pieces):
    flat = jnp.concatenate([f32(p).reshape(-1) for p in pieces])
    short = -flat.shape[0] % 1024
    return jnp.pad(flat, (0, short)).reshape(-1, 128)


def unpack(table, sizes):
    flat = table.reshape(table.shape[:-2] + (-1,))
    out, at = [], 0
    for size in sizes:
        out.append(flat[..., at : at + size])
        at += size
    return out


def softmax_parts(q, k, allowed):
    scores = jnp.einsum("hqc,hkc->hqk", q, k, preferred_element_type=F32) * SCALE
    masked = jnp.where(allowed[None], scores, MASKED)
    top = jnp.max(masked, axis=-1, keepdims=True)
    terms = jnp.where(allowed[None], jnp.exp(masked - top), 0.0)
    total = jnp.sum(terms, axis=-1, keepdims=True)
    return terms * (1.0 / total)


def attend(q, k, v, allowed):
    weights = softmax_parts(q, k, allowed)
    return jnp.einsum("hqk,hkc->hqc", low(weights), v, preferred_element_type=F32)


def attend_back(q, k, v, allowed, grad, attended):
    weights = softmax_parts(q, k, allowed)
    offset = jnp.sum(f32(grad) * attended, axis=-1)
    pushed = jnp.einsum("hqc,hkc->hqk", grad, v, preferred_element_type=F32)
    slopes = low(weights * (pushed - offset[..., None])) * BF16(SCALE)
    grad_q = jnp.einsum("hqk,hkc->hqc", slopes, k, preferred_element_type=F32)
    grad_k = jnp.einsum("hqk,hqc->hkc", slopes, q, preferred_element_type=F32)
    grad_v = jnp.einsum("hqk,hqc->hkc", low(weights), grad, preferred_element_type=F32)
    return grad_q, grad_k, grad_v


def heads_first(x):
    return x.transpose(1, 0, 2)


def heads_last(x):
    return x.transpose(1, 0, 2)


def allowed_pairs(query_codes, key_codes):
    return ((query_codes[:, None] >> 1) == (key_codes[None, :] >> 1)) & (
        (key_codes[None, :] & 1) == 1
    )


def shards(
    G,
    S,
    fields,
    patch_weight,
    variable_embed,
    query_vector,
    key_weight,
    value_weight,
    merge_weight,
    merge_bias,
    position_table,
    lead_weight,
    lead_bias,
    first_gain,
    first_shift,
    joint_weight,
    joint_bias,
    output_weight,
    output_bias,
    second_gain,
    second_shift,
    expand_weight,
    expand_bias,
    reduce_weight,
    reduce_bias,
    segment_ids,
    live_rows,
    lead_steps,
    cotangent,
):
    R = fields.shape[0]
    dn = value_weight.shape[0]
    fn = reduce_weight.shape[0]
    RG = G * R
    HL = HEADS // G
    CL = HL * HDIM
    FL = FF // G
    pairs = G * HL
    direct = pairs % S == 0 and HL % max(pairs // S, 1) == 0

    def swap(axis, *parts):
        return exchange(axis, parts)

    def gather_rows(w):
        return lax.all_gather(w, "seq", axis=0, tiled=True)

    merge_s = gather_rows(merge_weight)
    output_s = gather_rows(output_weight)

    table = jnp.concatenate(
        [patch_weight, variable_embed, jnp.zeros((KP - VP - VARS, dn), BF16)], axis=0
    )
    value_part = low(dot(value_weight, table, 0, 1)).reshape(G, CL, KP)
    key_part = low(dot(key_weight, table, 0, 1)).reshape(G, CL, KP)
    both = jnp.concatenate([value_part, key_part], axis=1)
    codes_own = segment_ids * 2 + live_rows
    vectors_own = [
        query_vector,
        merge_bias,
        lead_weight,
        lead_bias,
        first_gain,
        first_shift,
        output_bias,
        second_gain,
        second_shift,
        reduce_bias,
    ]
    small_own = pack([codes_own] + vectors_own)
    widen = (jnp.arange(VP)[:, None] == jnp.arange(KP)[None, :]).astype(BF16)
    column = jnp.arange(KP)
    field_own = low(dot(fields, widen, 1, 0) + ((column >= VP) & (column < VP + VARS)))
    joint_own = joint_weight.reshape(dn, 3, G, CL).transpose(2, 0, 1, 3).reshape(G, dn, 3 * CL)
    expand_own = expand_weight.reshape(dn, G, FL).transpose(1, 0, 2)
    both, joint_in, expand_in, field_in, position_in, small_in, cot_in = swap(
        "grp",
        (both, "each"),
        (joint_own, "each"),
        (expand_own, "each"),
        (field_own, "all"),
        (position_table, "all"),
        (small_own, "all"),
        (cotangent, "all"),
    )
    joint_s = (
        lax.all_gather(joint_in, "seq", axis=0, tiled=False)
        .transpose(1, 0, 2, 3)
        .reshape(D, 3 * CL)
    )
    expand_s = (
        lax.all_gather(expand_in, "seq", axis=0, tiled=False).transpose(1, 0, 2, 3).reshape(D, FL)
    )
    reduce_s = gather_rows(reduce_weight)
    field_rows = field_in.reshape(RG, KP)
    field_wide = dot(field_rows, (column[:, None] == column[None, :]).astype(BF16), 1, 0)
    cot_rows = cot_in.reshape(RG, D)
    position_rows = position_in.transpose(1, 0, 2).reshape(R, D)
    both = low(jnp.sum(f32(both), axis=0)).reshape(2, S, dn, KP).transpose(1, 0, 2, 3)
    small_rows = small_in.shape[0] * small_in.shape[1]
    slim = pack([joint_bias, expand_bias])
    both, small_all, slim_all = swap(
        "seq",
        (both.reshape(S, 2 * dn, KP), "each"),
        (small_in.reshape(small_rows, 128), "all"),
        (slim, "all"),
    )
    both = jnp.sum(f32(both), axis=0).reshape(2, dn, KP)
    value_own, key_own = both[0], both[1]
    probe_part = jnp.sum(key_own * f32(query_vector)[:, None], axis=0) * SCALE
    value_table, probe_parts = swap(
        "seq",
        (low(value_own), "all"),
        (jnp.broadcast_to(probe_part[None], (8, KP)), "all"),
    )
    value_table = value_table.reshape(CL, KP)
    probe_table = jnp.sum(probe_parts[:, 0].reshape(HL, S // HL, KP), axis=1)

    small_all = small_all.reshape(S, G, -1, 128)
    pieces = unpack(small_all, [R] + [dn] * len(vectors_own))
    codes = pieces[0].astype(jnp.int32)
    (
        full_query,
        full_merge_bias,
        full_lead,
        full_lead_bias,
        full_first_gain,
        full_first_shift,
        full_output_bias,
        full_second_gain,
        full_second_shift,
        full_reduce_bias,
    ) = [p.transpose(1, 0, 2).reshape(D) for p in pieces[1:]]
    joint_shift, expand_shift = unpack(slim_all, [2 * dn, fn])
    joint_shift = joint_shift.reshape(S, 2, dn).transpose(1, 0, 2).reshape(2, CL)
    expand_shift = expand_shift.reshape(FL)

    picked = jnp.where(
        segment_ids[:, None] == jnp.arange(lead_steps.shape[1])[None, :], lead_steps, 0
    )
    lead_rows = LEAD_UNIT * jnp.sum(picked, axis=1).astype(F32)

    owner = jnp.concatenate(
        [jnp.arange(VP) // PIX, jnp.arange(VARS), jnp.full((KP - VP - VARS,), VARS)]
    )
    select = (owner[:, None] == jnp.arange(VARS)[None, :]).astype(BF16)
    maps = probe_table[:, :, None] * f32(select)[None]
    maps_high = low(maps)
    maps_low = low(maps - f32(maps_high))
    scores = jnp.einsum("rk,hkv->hrv", field_rows, maps_high, preferred_element_type=F32)
    scores = scores + jnp.einsum("rk,hkv->hrv", field_rows, maps_low, preferred_element_type=F32)
    chosen = jax.nn.softmax(scores, axis=-1)
    spread = jnp.einsum("hrv,kv->hrk", low(chosen), select, preferred_element_type=F32)
    mixed = low(spread * field_wide[None])
    value_heads = value_table.reshape(HL, HDIM, KP)
    head_low = low(
        jnp.einsum("hrk,hck->rhc", mixed, value_heads, preferred_element_type=F32).reshape(RG, CL)
    )
    merged = low(dot(head_low, merge_s, 1, 0)).reshape(G, R, D)
    (merged,) = swap("grp", (merged, "each"))
    start = (
        jnp.sum(f32(merged), axis=0)
        + full_merge_bias
        + f32(position_rows)
        + lead_rows[:, None] * full_lead
        + full_lead_bias
    )
    start_hat, start_inv = norm_parts(start)
    (normed,) = swap("grp", (low(start_hat * full_first_gain + full_first_shift), "all"))
    normed = normed.reshape(RG, D)
    joint = dot(normed, joint_s, 1, 0)
    shift = jnp.concatenate([joint_shift[0], jnp.zeros((CL,), F32), joint_shift[1]])
    joint = low(joint + shift)

    if direct:
        per = pairs // S
        split = HL // per
        width = per * HDIM

        def to_pairs(x, kinds):
            x = x.reshape(G, R, kinds, split, width).transpose(0, 3, 1, 2, 4)
            (x,) = swap("seq", (x.reshape(S, R, kinds * width), "each"))
            return x.reshape(S * R, kinds, per, HDIM)

        def from_pairs(x, kinds):
            (x,) = swap("seq", (x.reshape(S, R, kinds * width), "each"))
            return (
                x.reshape(G, split, R, kinds, width)
                .transpose(0, 2, 3, 1, 4)
                .reshape(RG, kinds * CL)
            )

        mine = lax.axis_index("seq") // split
        pair_codes = lax.dynamic_index_in_dim(codes, mine, axis=1, keepdims=False).reshape(S * R)
        allowed = allowed_pairs(pair_codes, pair_codes)
        qkv = to_pairs(joint, 3)
        q, k, v = [heads_first(qkv[:, i]) for i in range(3)]
        attended = attend(q, k, v, allowed)
        attended_low = from_pairs(heads_last(low(attended)), 1)
    else:
        heads = joint.reshape(G, R, 3, HL, HDIM).transpose(0, 2, 3, 1, 4)
        everyone = lax.all_gather(heads[:, 1:], "seq", axis=3, tiled=True)
        all_codes = codes.transpose(1, 0, 2).reshape(G, S * R)
        my_codes = lax.dynamic_index_in_dim(codes, lax.axis_index("seq"), 0, keepdims=False)

        def forward_group(item):
            q, kv, query_codes, key_codes = item
            return attend(q, kv[0], kv[1], allowed_pairs(query_codes, key_codes))

        attended = lax.map(forward_group, (heads[:, 0], everyone, my_codes, all_codes))
        attended_low = low(attended).transpose(0, 2, 1, 3).reshape(RG, CL)

    branch = low(dot(attended_low, output_s, 1, 0)).reshape(G, R, D)
    (branch,) = swap("grp", (branch, "each"))
    middle = start + jnp.sum(f32(branch), axis=0) + full_output_bias
    middle_hat, middle_inv = norm_parts(middle)
    (second,) = swap("grp", (low(middle_hat * full_second_gain + full_second_shift), "all"))
    second = second.reshape(RG, D)
    hidden = dot(second, expand_s, 1, 0) + expand_shift
    inner = 0.7978845608028654 * (hidden + 0.044715 * hidden * hidden * hidden)
    bend = jnp.tanh(inner)
    active = low(0.5 * hidden * (1.0 + bend))
    slope = 0.5 * (1.0 + bend) + 0.5 * hidden * (1.0 - bend * bend) * 0.7978845608028654 * (
        1.0 + 3.0 * 0.044715 * hidden * hidden
    )
    reduced = low(dot(active, reduce_s, 1, 0)).reshape(G, R, D)

    grad_active = dot(cot_rows, reduce_s, 1, 1)
    grad_hidden = low(grad_active * slope)
    grad_second = low(dot(grad_hidden, expand_s, 1, 1)).reshape(G, R, D)
    grad_second, reduced = swap("grp", (grad_second, "each"), (reduced, "each"))
    activations = middle + jnp.sum(f32(reduced), axis=0) + full_reduce_bias
    grad_second = jnp.sum(f32(grad_second), axis=0)
    grad_top = f32(cotangent)
    grad_middle = grad_top + norm_back(middle_hat, middle_inv, full_second_gain, grad_second)
    grad_branch = low(grad_middle)

    def scatter_rows(w):
        return lax.psum_scatter(w, "seq", scatter_dimension=0, tiled=True)

    def scatter_mixed(w):
        cols = w.shape[1]
        w = w.reshape(G, S, dn, cols).transpose(1, 0, 2, 3).reshape(S, G * dn * cols // 1024, 1024)
        w = lax.psum_scatter(w, "seq", scatter_dimension=0, tiled=False)
        return w.reshape(G, dn, cols)

    grad_reduce_weight = f32(scatter_rows(low(dot(active, cot_rows, 0, 0))))
    grad_expand_mixed = scatter_mixed(low(dot(second, grad_hidden, 0, 0)))
    grad_expand_bias = low_sums(grad_hidden)

    (grad_branch_rows,) = swap("grp", (grad_branch, "all"))
    grad_branch_rows = grad_branch_rows.reshape(RG, D)
    grad_attended = low(dot(grad_branch_rows, output_s, 1, 1))
    grad_output_weight = f32(scatter_rows(low(dot(attended_low, grad_branch_rows, 0, 0))))
    if direct:
        pushed = heads_first(to_pairs(grad_attended, 1)[:, 0])
        grad_q, grad_k, grad_v = attend_back(q, k, v, allowed, pushed, attended)
        grads = [heads_last(low(x)) for x in (grad_q, grad_k, grad_v)]
        grad_joint = from_pairs(jnp.stack(grads, axis=1), 3)
    else:
        grad_heads = grad_attended.reshape(G, R, HL, HDIM).transpose(0, 2, 1, 3)

        def backward_group(item):
            q, kv, query_codes, key_codes, grad, done = item
            grad_q, grad_k, grad_v = attend_back(
                q, kv[0], kv[1], allowed_pairs(query_codes, key_codes), grad, done
            )
            return grad_q, jnp.stack([grad_k, grad_v], axis=0)

        grad_q, grad_kv = lax.map(
            backward_group,
            (heads[:, 0], everyone, my_codes, all_codes, grad_heads, attended),
        )
        grad_kv = lax.psum_scatter(grad_kv, "seq", scatter_dimension=3, tiled=True)
        grad_joint = low(jnp.concatenate([grad_q[:, None], grad_kv], axis=1))
        grad_joint = grad_joint.transpose(0, 3, 1, 2, 4).reshape(RG, 3 * CL)
    grad_normed = low(dot(grad_joint, joint_s, 1, 1)).reshape(G, R, D)
    (grad_normed,) = swap("grp", (grad_normed, "each"))
    grad_normed = jnp.sum(f32(grad_normed), axis=0)
    grad_joint_mixed = scatter_mixed(low(dot(normed, grad_joint, 0, 0)))
    joint_sums = low_sums(grad_joint)
    grad_start = grad_middle + norm_back(start_hat, start_inv, full_first_gain, grad_normed)
    grad_merged = low(grad_start)

    grad_merged_rows, grad_joint_in, grad_expand_in = swap(
        "grp", (grad_merged, "all"), (grad_joint_mixed, "each"), (grad_expand_mixed, "each")
    )
    grad_joint_weight = f32(
        grad_joint_in.reshape(G, dn, 3, CL).transpose(1, 2, 0, 3).reshape(dn, 3 * D)
    )
    grad_expand_weight = f32(grad_expand_in.transpose(1, 0, 2).reshape(dn, FF))
    grad_merged_rows = grad_merged_rows.reshape(RG, D)
    grad_head = low(dot(grad_merged_rows, merge_s, 1, 1))
    grad_merge_weight = f32(scatter_rows(low(dot(head_low, grad_merged_rows, 0, 0))))
    grad_heads_low = grad_head.reshape(RG, HL, HDIM)
    value_back = jnp.einsum(
        "rhc,hck->hrk", grad_heads_low, value_heads, preferred_element_type=F32
    )
    weighed = value_back * field_wide[None]
    weighed_high = low(weighed)
    weighed_low = low(weighed - f32(weighed_high))
    grad_chosen = jnp.einsum("hrk,kv->hrv", weighed_high, select, preferred_element_type=F32)
    grad_chosen = grad_chosen + jnp.einsum(
        "hrk,kv->hrv", weighed_low, select, preferred_element_type=F32
    )
    grad_scores = low(
        chosen * (grad_chosen - jnp.sum(chosen * grad_chosen, axis=-1, keepdims=True))
    )
    score_spread = jnp.einsum("hrv,kv->hrk", grad_scores, select, preferred_element_type=F32)
    field_part = jnp.sum(spread * value_back + score_spread * probe_table[:, None, :], axis=0)
    field_part = field_part.reshape(G, R, KP)
    score_sums = jnp.sum(score_spread * field_wide[None], axis=1)
    head_sums = jnp.einsum(
        "rhc,hrk->hck", grad_heads_low, mixed, preferred_element_type=F32
    ).reshape(S, dn, KP)

    column_sums = jnp.stack(
        [
            low_sums(grad_merged),
            jnp.sum(lead_rows[:, None] * grad_start, axis=0),
            jnp.sum(grad_start, axis=0),
            jnp.sum(grad_normed * start_hat, axis=0),
            jnp.sum(grad_normed, axis=0),
            low_sums(grad_branch),
            jnp.sum(grad_second * middle_hat, axis=0),
            jnp.sum(grad_second, axis=0),
            jnp.sum(grad_top, axis=0),
        ]
    )
    kinds = column_sums.shape[0]
    column_sums = jnp.pad(column_sums, ((0, -kinds % 16), (0, 0)))
    column_sums = column_sums.reshape(-1, G, CL).transpose(1, 0, 2)
    position_blocks = grad_merged.reshape(R, G, CL).transpose(1, 0, 2)
    column_sums, position_blocks, field_part = swap(
        "grp", (column_sums, "each"), (position_blocks, "each"), (field_part, "each")
    )
    grad_position_table = jnp.sum(f32(position_blocks), axis=0)
    field_grad = jnp.sum(field_part, axis=0)[:, :VP]
    column_sums = jnp.sum(column_sums, axis=0)
    team_sums = jnp.concatenate(
        [
            column_sums[:kinds].reshape(kinds, S, dn).transpose(1, 0, 2).reshape(S, kinds * dn),
            joint_sums[:CL].reshape(S, dn),
            joint_sums[2 * CL :].reshape(S, dn),
            grad_expand_bias.reshape(S, fn),
        ],
        axis=1,
    )
    wide = team_sums.shape[1]
    team_sums = jnp.pad(team_sums, ((0, 0), (0, -wide % 1024))).reshape(S, -1, 128)
    score_sums = jnp.pad(score_sums, ((0, -HL % 8), (0, 0)))
    team_sums, head_sums, score_sums = swap(
        "seq", (team_sums, "each"), (low(head_sums), "each"), (score_sums, "all")
    )
    team_sums = jnp.sum(team_sums, axis=0).reshape(-1)[:wide]
    own_sums = team_sums[: kinds * dn].reshape(kinds, dn)
    grad_joint_bias = team_sums[kinds * dn : (kinds + 2) * dn].reshape(2, dn)
    grad_expand_bias = team_sums[(kinds + 2) * dn :]
    (
        grad_merge_bias,
        grad_lead_weight,
        grad_lead_bias,
        grad_first_gain,
        grad_first_shift,
        grad_output_bias,
        grad_second_gain,
        grad_second_shift,
        grad_reduce_bias,
    ) = [own_sums[i] for i in range(kinds)]
    head_sums = jnp.sum(f32(head_sums), axis=0)
    score_sums = jnp.sum(score_sums, axis=0)
    my_head = lax.axis_index("seq") * dn // HDIM
    my_scores = lax.dynamic_index_in_dim(score_sums, my_head, axis=0, keepdims=False)
    grad_query_vector = jnp.sum(key_own * my_scores[None], axis=1) * SCALE
    (head_all,) = swap("seq", (low(head_sums), "all"))
    head_all, score_all = swap(
        "grp", (head_all.reshape(S * dn, KP), "all"), (score_sums, "all")
    )
    head_all = head_all.reshape(D, KP)
    score_all = score_all[:, :HL].reshape(HEADS, KP)
    grad_value_weight = dot(table, head_all, 0, 1)
    probe_own = low(
        jnp.sum((f32(key_weight) * full_query).reshape(dn, HEADS, HDIM), axis=-1) * SCALE
    )
    grad_table = dot(head_all, value_weight, 0, 1)
    grad_table = grad_table + jnp.einsum("hk,dh->kd", score_all, f32(probe_own))
    grad_probe = jnp.einsum("kd,hk->dh", f32(table), score_all)
    grad_key_weight = (
        grad_probe[:, :, None] * full_query.reshape(HEADS, HDIM)[None] * SCALE
    ).reshape(dn, D)
    grad_patch_weight = grad_table[:VP]
    grad_variable_embed = grad_table[VP : VP + VARS]
    return (
        activations,
        field_grad,
        grad_patch_weight,
        grad_variable_embed,
        grad_query_vector,
        grad_key_weight,
        grad_value_weight,
        grad_merge_weight,
        grad_merge_bias,
        grad_position_table,
        grad_lead_weight,
        grad_lead_bias,
        grad_first_gain,
        grad_first_shift,
        grad_joint_weight,
        grad_joint_bias,
        grad_output_weight,
        grad_output_bias,
        grad_second_gain,
        grad_second_shift,
        grad_expand_weight,
        grad_expand_bias,
        grad_reduce_weight,
        grad_reduce_bias,
    )


TEAM = 4
LINE = 8
ROW = 128
TALL = TEAM * ROW
GROUP = LINE * ROW
WD = D // (TEAM * LINE)
QC = D // TEAM
TEAM_HEADS = HEADS // TEAM
PACKED = 4
VECTORS = 12
QUERY, MERGE_BIAS, LEAD_WEIGHT, LEAD_BIAS, FIRST_GAIN, FIRST_SHIFT = range(6)
OUTPUT_BIAS, SECOND_GAIN, SECOND_SHIFT, REDUCE_BIAS = range(6, 10)
SUM_ROWS = 16

INPUTS = dict(
    fields=pltpu.VMEM,
    patch=pltpu.VMEM,
    embed=pltpu.VMEM,
    key_w=pltpu.VMEM,
    value_w=pltpu.VMEM,
    pack=pltpu.VMEM,
    joint_b=pltpu.VMEM,
    segments=pltpu.VMEM,
    live=pltpu.VMEM,
    steps=pltpu.SMEM,
    cot=pl.ANY,
    position=pl.ANY,
    joint_w=pl.ANY,
    expand_w=pl.ANY,
    merge_w=pl.ANY,
    output_w=pl.ANY,
    reduce_w=pl.ANY,
)

OUTPUTS = dict(
    activations=((ROW, D), F32),
    field_grad=((VP, ROW), F32),
    g_patch=((WD, VP), F32),
    g_embed=((WD, VARS), F32),
    g_key=((WD, D), F32),
    g_value=((WD, D), F32),
    g_merge=((WD, D), F32),
    g_position=((ROW, QC), F32),
    g_joint=((WD, 3 * D), F32),
    g_output=((WD, D), F32),
    g_expand=((WD, FF), F32),
    g_reduce=((ROW, D), F32),
    small=((32, 128), F32),
)

SCRATCH = dict(
    head_all=((TEAM, LINE, WD, KP), BF16),
    score_all=((TEAM, 8, KP), F32),
    score_rows=((16, KP), F32),
    key_own=((WD, KP), F32),
    sums=((SUM_ROWS, QC), F32),
    pe=((WD, KP), BF16),
    field_all=((TEAM, ROW, KP), BF16),
    pos=((ROW, D), BF16),
    cot_all=((TEAM, ROW, D), BF16),
    pack_rows=((16, 128), F32),
    pack_all=((LINE, TEAM, 16, 128), BF16),
    vecs=((16, D), F32),
    shift_e=((8, D), F32),
    seg_q=((16, GROUP), BF16),
    seg_k=((16, GROUP), BF16),
    merge_s=((LINE, WD, D), BF16),
    output_s=((LINE, WD, D), BF16),
    reduce_s=((LINE, ROW, D), BF16),
    joint_s=((TEAM, LINE, WD, 3 * QC), BF16),
    expand_s=((TEAM, LINE, WD, D), BF16),
    e2_send=((2, LINE, WD, KP), BF16),
    e2_recv=((LINE, 2, WD, KP), BF16),
    pv=((LINE, WD, KP), BF16),
    at=((LINE, 8, KP), F32),
    probe=((8, KP), F32),
    select=((KP, 128), BF16),
    select_t=((128, KP), BF16),
    chosen=((TEAM_HEADS, TALL, 128), F32),
    head_low=((TALL, QC), BF16),
    start=((ROW, D), F32),
    start_hat=((ROW, D), F32),
    start_inv=((ROW, 128), F32),
    middle=((ROW, D), F32),
    middle_hat=((ROW, D), F32),
    middle_inv=((ROW, 128), F32),
    grad_mid=((ROW, D), F32),
    normed_all=((TEAM, ROW, D), BF16),
    second_all=((TEAM, ROW, D), BF16),
    gb_all=((TEAM, ROW, D), BF16),
    gm_all=((TEAM, ROW, D), BF16),
    pair_send=((LINE, 3, ROW, 128), BF16),
    qkv=((3, GROUP, 128), BF16),
    p_low=((2, GROUP, GROUP), BF16),
    att_f=((GROUP, 128), F32),
    att_low=((GROUP, 128), BF16),
    att_all=((TEAM, ROW, QC), BF16),
    g_send=((TEAM, 2, ROW, 128), BF16),
    go=((GROUP, 128), BF16),
    dq=((GROUP, 128), F32),
    d_all=((TEAM, 3, ROW, QC), BF16),
    active_all=((TEAM, ROW, D), BF16),
    gh_all=((TEAM, ROW, D), BF16),
    own_a=((ROW, D), F32),
    own_b=((ROW, D), F32),
    far_a=((ROW, D), F32),
    far_b=((ROW, D), F32),
    far_d=((ROW, D), F32),
    gw_merge=((LINE, WD, D), BF16),
    gw_output=((LINE, WD, D), BF16),
    gw_reduce=((LINE, ROW, D), BF16),
    gw_joint=((TEAM, LINE, WD, 3 * QC), BF16),
    gw_expand=((TEAM, LINE, WD, D), BF16),
    yr_merge=((4, WD, D), BF16),
    yr_output=((4, WD, D), BF16),
    yr_reduce=((4, ROW // 2, D), BF16),
    yr_half=((1, ROW // 2, D), BF16),
    zr_half=((6, ROW // 2, D), BF16),
    za_half=((4, ROW // 2, D), BF16),
    yr_joint=((4, TEAM, WD, 3 * QC), BF16),
    yr_expand=((4, TEAM, WD, D), BF16),
    zr_merge=((3, WD, D), BF16),
    za_merge=((2, WD, D), BF16),
    zr_output=((3, WD, D), BF16),
    za_output=((2, WD, D), BF16),
    zr_reduce=((3, ROW // 2, D), BF16),
    za_reduce=((2, ROW // 2, D), BF16),
    zr_joint=((3, TEAM, WD, 3 * QC), BF16),
    za_joint=((2, TEAM, WD, 3 * QC), BF16),
    zr_expand=((3, TEAM, WD, D), BF16),
    za_expand=((2, TEAM, WD, D), BF16),
    xs_joint=((TEAM, WD, 3 * QC), BF16),
    xs_expand=((TEAM, WD, D), BF16),
    xr_joint=((TEAM, WD, 3 * QC), BF16),
    xr_expand=((TEAM, WD, D), BF16),
    csum=((16, D), F32),
    crecv=((TEAM, 16, QC), F32),
    tsum=((LINE, SUM_ROWS, QC), F32),
    f_own=((TEAM, ROW, KP), F32),
    f_recv=((3, ROW, KP), F32),
    t_send=((LINE, WD, KP), BF16),
    t_recv=((LINE, WD, KP), BF16),
    q_all=((LINE, 8, KP), F32),
)

TEAM_SUMS = dict(
    both=(2 * QC, KP),
    merge=(ROW, D),
    branch=(ROW, D),
    second=(ROW, D),
    reduced=(ROW, D),
    normed=(ROW, D),
)


def team_sum_buffers(shape):
    near = ((2,) + shape, BF16)
    one = (shape, BF16)
    return (near, near, one, one)


SEMAPHORES = 252


def nn(a, b):
    return dot(a, b, 1, 0)


def nt(a, b):
    return dot(a, b, 1, 1)


def tn(a, b):
    return dot(a, b, 0, 0)


def lanes(at, size):
    return pl.ds(pl.multiple_of(at, 128), size)


def rows(at, size):
    return pl.ds(pl.multiple_of(at, size), size)


def fused_kernel(*refs):
    n_in, n_out = len(INPUTS), len(OUTPUTS)
    results = types.SimpleNamespace(**dict(zip(OUTPUTS, refs[n_in : n_in + n_out])))
    names = list(INPUTS) + list(SCRATCH) + list(OUTPUTS)
    rest = refs[:n_in] + refs[n_in + n_out :]
    ref = types.SimpleNamespace(**dict(zip(names, rest)))
    rest = rest[len(names) :]
    send, recv = rest[-2:]
    sums = dict(zip(TEAM_SUMS, [rest[4 * i : 4 * i + 4] for i in range(len(TEAM_SUMS))]))
    sums = types.SimpleNamespace(**sums)
    g = lax.axis_index("grp")
    s = lax.axis_index("seq")
    sib = g + 1 - 2 * lax.rem(g, 2)
    far = lax.rem(g + 2, TEAM)
    diag = lax.rem(sib + 2, TEAM)
    z = s // 2
    y = s - 2 * z
    beside = s + 1 - 2 * y
    mine = lax.rem(3 * z, TEAM)
    is_middle = (z == 1) | (z == 2)
    is_end = (z == 0) | (z == 3)
    partner = s + 2 - 4 * lax.rem(z, 2)
    facing = lax.rem(s + 6 - 4 * z + LINE, LINE)
    near_places = [4 * (z // 2) + y + 2 * i for i in range(2)]
    far_places = [4 * (1 - z // 2) + y + 2 * i for i in range(2)]

    def to_team(j):
        return (j, s)

    def to_line(j):
        return (g, j)

    used = [0]
    begun = []

    def reserve(count):
        at = used[0]
        used[0] += count
        assert used[0] <= SEMAPHORES
        return at

    def remote(src, dst, device, at):
        return pltpu.make_async_remote_copy(
            src_ref=src,
            dst_ref=dst,
            send_sem=send.at[at],
            recv_sem=recv.at[at],
            device_id=device,
            device_id_type=MESH,
        )

    def push(src, dst, device):
        copy = remote(src, dst, device, reserve(1))
        copy.start()
        begun.append(copy)
        return copy

    barrier = pltpu.get_barrier_semaphore()
    for step in range(1, TEAM):
        pl.semaphore_signal(
            barrier, inc=1, device_id=to_team(lax.rem(g + step, TEAM)), device_id_type=MESH
        )
    for step in range(1, LINE):
        pl.semaphore_signal(
            barrier, inc=1, device_id=to_line(lax.rem(s + step, LINE)), device_id_type=MESH
        )

    class Together:
        def __init__(self, bulk, waits_itself=False):
            self.bulk, self.at = bulk, reserve(1)
            if not waits_itself:
                begun_together.append(self)

        def push(self, src, dst, device):
            remote(src, dst, device, self.at).start()

        def wait_recv(self):
            remote(self.bulk, self.bulk, to_line(beside), self.at).wait_recv()

        def wait_send(self):
            remote(self.bulk, self.bulk, to_line(beside), self.at).wait_send()

    begun_together = []

    def spread(buf):
        half = buf.shape[1] // 2
        across = []
        for h in range(2):
            part = buf.at[g, pl.ds(h * half, half)]
            across.append(push(part, part, to_team(far)))
        return push(buf.at[g], buf.at[g], to_team(sib)), across

    def spread_on(buf, across):
        half = buf.shape[1] // 2
        handed = Together(buf.at[far])
        for h in range(2):
            across[h].wait_recv()
            part = buf.at[far, pl.ds(h * half, half)]
            handed.push(part, part, to_team(sib))
        return [handed]

    def wait_all(copies):
        for copy in copies:
            copy.wait_recv()

    class TeamSum:
        def __init__(self, buffers):
            self.ps, self.r, self.t, self.x = buffers
            self.near_copies = [None, None]

        def near(self, slot, value=None):
            if value is not None:
                self.ps[slot] = low(value)
            self.near_copies[slot] = push(self.ps.at[slot], self.r.at[slot], to_team(sib))

        def across(self, value):
            self.near_copies[1].wait_recv()
            half = self.t.shape[0] // 2
            self.far_copies = [Together(self.x)]
            for h in range(2):
                part = pl.ds(h * half, half)
                self.t[part] = low(value(part) + f32(self.r[1, part]))
                self.far_copies[0].push(self.t.at[part], self.x.at[part], to_team(far))

        def total(self, own):
            self.near_copies[0].wait_recv()
            wait_all(self.far_copies)
            return own + f32(self.r[0]) + f32(self.x[...])

    deposits = []

    def deposit(src, dst):
        copy = pltpu.make_async_copy(src, dst, recv.at[reserve(1)])
        copy.start()
        deposits.append(copy)

    def to_whole_line(src, dst, bulk):
        group = Together(bulk)
        for step in range(1, LINE):
            place = lax.rem(s + step, LINE)
            group.push(src(place), dst, to_line(place))
        return [group]

    def share_line(buf):
        return to_whole_line(lambda place: buf.at[s], buf.at[s], buf.at[pl.ds(0, LINE - 1)])

    def to_whole_team(src, dst, bulk):
        group = Together(bulk)
        for j in (far, diag, sib):
            group.push(src(j), dst, to_team(j))
        return [group]

    def mean(x):
        return jnp.sum(x, axis=-1, keepdims=True) * (1.0 / D)

    class Gather:
        def __init__(self, slot):
            self.slot = slot
            self.at = reserve(9)

        def send(self, place, device, i, shard=None):
            part = self.slot(place)
            remote(part if shard is None else shard, part, device, self.at + i).start()

        def come(self, i):
            part = self.slot(s)
            remote(part, part, to_line(beside), self.at + i).wait_recv()

        def stage1(self, shard=None):
            self.send(s, to_line(partner), 0, shard)
            self.send(s, to_line(beside), 1, shard)

        def stage2(self, hold=False):
            self.come(0)

            @pl.when(is_middle)
            def _():
                for i in range(2):
                    self.send(near_places[i], to_line(facing), 2 + i)

            if not hold:
                self.hand_on()

        def hand_on(self):
            self.send(partner, to_line(beside), 4)

        def stage3(self):
            @pl.when(is_middle)
            def _():
                for i in range(2):
                    self.come(2 + i)
                    self.send(far_places[i], to_line(partner), 5 + i)
                    self.send(far_places[i], to_line(beside), 7 + i)

        def stage4(self):
            @pl.when(is_end)
            def _():
                for i in range(2):
                    self.come(5 + i)
                    self.send(far_places[i], to_line(beside), 7 + i)

        def finish(self):
            for i in (1, 4, 7, 8):
                self.come(i)

        def sent(self):
            part = self.slot(s)

            def gone(i):
                remote(part, part, to_line(beside), self.at + i).wait_send()

            for i in (0, 1, 4, 7, 8):
                gone(i)

            @pl.when(is_middle)
            def _():
                for i in (2, 3, 5, 6):
                    gone(i)

    class PairExchange:
        def __init__(self, bulk):
            self.group, self.own = Together(bulk, waits_itself=True), reserve(1)

        def send(self, src, dst, there):
            @pl.when(there != s)
            def _():
                self.group.push(src, dst, to_line(there))

            @pl.when(there == s)
            def _():
                pltpu.make_async_copy(src, dst, recv.at[self.own]).start()

        def wait(self, src, dst):
            pltpu.make_async_copy(src, dst, recv.at[self.own]).wait()
            self.group.wait_recv()
            self.group.wait_send()

    pe = ref.pe
    pe[:, 0:VP] = ref.patch[...]
    pe[:, VP : VP + VARS] = ref.embed[...]
    pe[:, VP + VARS :] = jnp.zeros((WD, KP - VP - VARS), BF16)
    field_all, cot_all, pack_all = ref.field_all, ref.cot_all, ref.pack_all
    field_all[g, :, 0:VP] = ref.fields[...].T
    lane = lax.broadcasted_iota(jnp.int32, (ROW, KP - VP), 1)
    field_all[g, :, VP:] = (lane < VARS).astype(BF16)
    pack_rows = ref.pack_rows
    pack_rows[...] = f32(ref.pack[...])
    for i in range(2):
        pack_rows[2:3, 64 + i * WD : 64 + (i + 1) * WD] = f32(ref.joint_b[...])[i : i + 1]
    pack_rows[4:5] = ref.segments[...].astype(F32)
    pack_rows[5:6] = ref.live[...].astype(F32)
    pack_all[s, g] = low(pack_rows[...])
    pl.semaphore_wait(barrier, TEAM - 1 + LINE - 1)

    both = TeamSum(sums.both)

    def table_product(weight, j):
        return tn(weight[:, lanes(j * QC, QC)], pe[...])

    for slot, j in ((1, diag), (0, sib)):
        both.ps[slot, 0:QC] = low(table_product(ref.value_w, j))
        both.ps[slot, QC:] = low(table_product(ref.key_w, j))
        both.near(slot)
    field_copies = spread(field_all)
    far_parts = [table_product(ref.value_w, far), table_product(ref.key_w, far)]
    both.across(lambda part: far_parts[0] if part.start == 0 else far_parts[1])
    own_parts = [table_product(ref.value_w, g), table_product(ref.key_w, g)]
    pack_here = pack_all.at[s, g]
    pack_copies = to_whole_team(lambda j: pack_here, pack_here, pack_all.at[0, pl.ds(0, 3)])

    def whole(buf):
        return lambda i: buf.at[i]

    def inner(buf):
        return lambda i: buf.at[:, i]

    def some_rows(buf, at, size):
        return lambda i: buf.at[i, pl.ds(at, size)]

    def some_lanes(buf, at, size):
        return lambda i: buf.at[:, i, :, pl.ds(at, size)]

    half_rows, half_lanes = ROW // 2, D // 2
    gather_merge = Gather(whole(ref.merge_s))
    gather_output = Gather(whole(ref.output_s))
    gather_reduce = [Gather(some_rows(ref.reduce_s, i * half_rows, half_rows)) for i in range(2)]
    gather_joint = [Gather(some_lanes(ref.joint_s, i * QC, QC)) for i in range(3)]
    gather_expand = [Gather(some_lanes(ref.expand_s, i * half_lanes, half_lanes)) for i in range(2)]
    local = []

    def keep(src, dst):
        copy = pltpu.make_async_copy(src, dst, recv.at[reserve(1)])
        copy.start()
        local.append(copy)

    keep(ref.merge_w, ref.merge_s.at[s])
    keep(ref.output_w, ref.output_s.at[s])
    keep(ref.reduce_w, ref.reduce_s.at[s])
    keep(ref.cot, cot_all.at[g])
    gather_merge.stage1(ref.merge_w)
    for i in range(2):
        gather_reduce[i].stage1(ref.reduce_w.at[pl.ds(i * half_rows, half_rows)])

    joint_copies = [Together(ref.joint_s.at[pl.ds(0, 3), 0])]
    for j in (far, diag, sib):
        for kind in range(3):
            joint_copies[0].push(
                ref.joint_w.at[:, lanes(kind * D + j * QC, QC)],
                ref.joint_s.at[g, s, :, pl.ds(kind * QC, QC)],
                to_team(j),
            )
    for kind in range(3):
        keep(
            ref.joint_w.at[:, lanes(kind * D + g * QC, QC)],
            ref.joint_s.at[g, s, :, pl.ds(kind * QC, QC)],
        )
    expand_copies = to_whole_team(
        lambda j: ref.expand_w.at[:, lanes(j * D, D)],
        ref.expand_s.at[g, s],
        ref.expand_s.at[pl.ds(0, 3), 0],
    )
    keep(ref.expand_w.at[:, lanes(g * D, D)], ref.expand_s.at[g, s])
    keep(ref.position, ref.pos.at[:, lanes(g * QC, QC)])
    position_copies = to_whole_team(
        lambda j: ref.position, ref.pos.at[:, lanes(g * QC, QC)], ref.pos.at[:, pl.ds(0, 3 * QC)]
    )

    for copy in local:
        copy.wait()
    gather_merge.stage2()

    both.near_copies[0].wait_recv()
    wait_all(both.far_copies)
    for part in range(2):
        block = pl.ds(part * QC, QC)
        total = own_parts[part] + f32(both.r[0, block]) + f32(both.x[block])
        ref.e2_send[part] = low(total).reshape(LINE, WD, KP)
    e2_send, e2_recv = ref.e2_send, ref.e2_recv
    e2_copies = to_whole_line(
        lambda place: e2_send.at[:, place], e2_recv.at[s], e2_recv.at[pl.ds(0, LINE - 1)]
    )
    e2_recv[s] = e2_send[:, s]
    wait_all(joint_copies)
    for gather in gather_joint:
        gather.stage1()
    gather_merge.stage3()

    wait_all(e2_copies)
    table_own = jnp.sum(f32(e2_recv[...]), axis=0)
    key_own = table_own[1]
    ref.key_own[...] = key_own
    query = f32(pack_all[s, g])[0:1, 0:WD]
    key_high = low(key_own)
    key_rest = low(key_own - f32(key_high))
    query_rows = low(jnp.broadcast_to(query, (16, WD)))
    probe_part = (nn(query_rows, key_high) + nn(query_rows, key_rest)) * SCALE
    pv, at = ref.pv, ref.at
    pv[s] = low(table_own[0])
    at[s] = probe_part[0:8]
    pv_copies = share_line(pv)
    at_copies = to_whole_line(
        lambda place: at.at[s, pl.ds(0, 1)],
        at.at[s, pl.ds(0, 1)],
        at.at[pl.ds(0, LINE - 1), pl.ds(0, 1)],
    )
    for gather in gather_joint:
        gather.stage2()
    wait_all(pv_copies)
    wait_all(at_copies)
    gather_merge.stage4()
    wait_all(pack_copies)
    pack_line = share_line(pack_all)
    wait_all(expand_copies)
    for gather in gather_expand:
        gather.stage1()

    probe = ref.probe
    for h in range(TEAM_HEADS):
        probe[h : h + 1] = at[2 * h, 0:1] + at[2 * h + 1, 0:1]
    probe[TEAM_HEADS:] = jnp.zeros((8 - TEAM_HEADS, KP), F32)

    def owner_of(k):
        return jnp.where(k < VP, k // PIX, jnp.where(k < VP + VARS, k - VP, VARS + 64))

    select, select_t = ref.select, ref.select_t
    select[...] = (
        owner_of(lax.broadcasted_iota(jnp.int32, (KP, 128), 0))
        == lax.broadcasted_iota(jnp.int32, (KP, 128), 1)
    ).astype(BF16)
    select_t[...] = (
        owner_of(lax.broadcasted_iota(jnp.int32, (128, KP), 1))
        == lax.broadcasted_iota(jnp.int32, (128, KP), 0)
    ).astype(BF16)
    valid = lax.broadcasted_iota(jnp.int32, (1, 128), 1) < VARS
    head_of_lane = lax.broadcasted_iota(jnp.int32, (1, QC), 1) // HDIM

    field_handed = spread_on(field_all, field_copies[1])
    field_copies[0].wait_recv()
    wait_all(field_handed)

    def tall(buf):
        return buf[...].reshape(TALL, -1)

    def split_dot(x, b):
        high = low(x)
        return nn(high, b) + nn(low(x - f32(high)), b)

    chosen, head_low = ref.chosen, ref.head_low

    def choose(h):
        field = f32(tall(field_all))
        scores = split_dot(field * probe[h : h + 1], select[...])
        scores = jnp.where(valid, scores, MASKED)
        terms = jnp.exp(scores - jnp.max(scores, axis=-1, keepdims=True))
        weights = terms * (1.0 / jnp.sum(terms, axis=-1, keepdims=True))
        chosen[h] = weights
        mix = low(nn(low(weights), select_t[...]) * field)
        table_value = pv[2 * h : 2 * h + 2].reshape(HDIM, KP)
        head_low[:, h * HDIM : (h + 1) * HDIM] = low(nt(mix, table_value))

    for h in range(TEAM_HEADS):
        choose(h)

    merge_s, output_s = ref.merge_s, ref.output_s
    gather_merge.finish()
    merge = TeamSum(sums.merge)

    def row_weight(buf):
        return buf[...].reshape(-1, D)

    def two(buf, i, j):
        return jnp.concatenate([buf[i], buf[j]], axis=0)

    def merge_part(j):
        return nn(head_low[rows(j * ROW, ROW)], row_weight(merge_s))

    merge.near(1, merge_part(diag))
    ref.far_a[...] = merge_part(far)
    merge.across(lambda part: ref.far_a[part])
    merge.near(0, merge_part(sib))
    ref.own_a[...] = merge_part(g)

    wait_all(pack_line)
    vecs, shift_e = ref.vecs, ref.shift_e
    lane_piece = lax.broadcasted_iota(jnp.int32, (LINE, 1, QC), 2) // WD
    piece = lax.broadcasted_iota(jnp.int32, (LINE, 1, QC), 0)
    for q in range(PACKED):
        place = (
            lax.broadcasted_iota(jnp.int32, (128, QC), 1) % WD + q * WD
            == lax.broadcasted_iota(jnp.int32, (128, QC), 0)
        ).astype(BF16)
        for j in range(TEAM):
            spreadout = nn(pack_all[:, j].reshape(LINE * 16, 128), place)
            spreadout = jnp.where(lane_piece == piece, spreadout.reshape(LINE, 16, QC), 0.0)
            spreadout = jnp.sum(spreadout, axis=0)
            vecs[4 * q : 4 * q + 4, j * QC : (j + 1) * QC] = spreadout[0:4]

    def vector(i):
        at_row = 4 * (i % PACKED) + i // PACKED
        return vecs[at_row : at_row + 1, :]

    joint_shift = [
        vecs[4 * (i % PACKED) + i // PACKED, lanes(g * QC, QC)].reshape(1, QC) for i in (10, 11)
    ]
    seg_q, seg_k = ref.seg_q, ref.seg_k
    sub = lax.broadcasted_iota(jnp.int32, (16, 128), 0).astype(F32)
    for j in range(LINE):
        part = f32(pack_all[j, g])
        shift_e[:, j * 128 : (j + 1) * 128] = jnp.broadcast_to(part[3:4], (8, 128))
        part = f32(pack_all[j, mine])
        same = jnp.where(sub == part[4:5], 1.0, 0.0)
        seg_q[:, j * 128 : (j + 1) * 128] = low(same)
        seg_k[:, j * 128 : (j + 1) * 128] = low(same * part[5:6])
    own_seg = ref.segments[...].astype(F32)
    steps = ref.steps
    lead_lanes = jnp.zeros((1, 128), F32)
    for i in range(steps.shape[1]):
        lead_lanes = jnp.where(own_seg == i, LEAD_UNIT * steps[0, i].astype(F32), lead_lanes)
    lead = jnp.broadcast_to(lead_lanes, (ROW, 128)).T[:, 0:1]
    wait_all(position_copies)
    for gather in gather_joint:
        gather.stage3()
    gather_output.stage1(ref.output_w)
    for gather in gather_reduce:
        gather.stage2(hold=True)

    start_ref = ref.start
    start_ref[...] = (
        merge.total(ref.own_a[...])
        + vector(MERGE_BIAS)
        + f32(ref.pos[...])
        + lead * vector(LEAD_WEIGHT)
        + vector(LEAD_BIAS)
    )

    def norm(x, hat_ref, inv_ref, gain, shift):
        center = x - mean(x)
        inverse = lax.rsqrt(mean(center * center) + EPSILON)
        hat = center * inverse
        hat_ref[...] = hat
        inv_ref[...] = jnp.broadcast_to(inverse, (ROW, 128))
        return low(hat * gain + shift)

    def norm_back_ref(grad, hat_ref, inv_ref, gain):
        f = grad * gain
        hat = hat_ref[...]
        return inv_ref[:, 0:1] * (f - mean(f) - hat * mean(f * hat))

    normed_all = ref.normed_all
    normed_all[g] = norm(
        start_ref[...],
        ref.start_hat,
        ref.start_inv,
        vector(FIRST_GAIN),
        vector(FIRST_SHIFT),
    )
    normed_copies = spread(normed_all)
    joint_s, pair_send, qkv = ref.joint_s, ref.pair_send, ref.qkv
    for gather in gather_joint:
        gather.stage4()
    e6 = [PairExchange(qkv.at[kind, pl.ds(0, 7 * ROW), :]) for kind in range(3)]

    def pair_place(j, t):
        return 2 * lax.rem(3 * j, TEAM) + t

    line_rows = rows(s * ROW, ROW)

    def joint_rows(i, j):
        block = two(normed_all, i, j)
        for kind in range(3):
            if i is g:
                gather_joint[kind].finish()
            weight = joint_s[:, :, :, kind * QC : (kind + 1) * QC].reshape(D, QC)
            part = nn(block, weight)
            if kind != 1:
                part = part + joint_shift[kind // 2]
            part = low(part)
            for n, group in enumerate((i, j)):
                for t in range(2):
                    place = pair_place(group, t)
                    pair_send[place, kind] = part[n * ROW : (n + 1) * ROW, t * 128 : (t + 1) * 128]
                    e6[kind].send(pair_send.at[place, kind], qkv.at[kind, line_rows, :], place)

    normed_copies[0].wait_recv()
    joint_rows(g, sib)
    normed_handed = spread_on(normed_all, normed_copies[1])
    wait_all(normed_handed)
    joint_rows(far, diag)
    gather_output.stage2()
    gather_expand[0].stage2()
    for gather in gather_reduce:
        gather.hand_on()
        gather.stage3()
    for kind in range(3):
        e6[kind].wait(pair_send.at[0, kind], qkv.at[kind, line_rows, :])
    gather_output.stage3()
    gather_expand[1].stage2()
    cot_copies = spread(cot_all)

    half_of_lane = lax.broadcasted_iota(jnp.int32, (1, 128), 1) // HDIM
    p_low, att_f, att_low, att_all = ref.p_low, ref.att_f, ref.att_low, ref.att_all
    e7 = PairExchange(att_low.at[pl.ds(0, 7 * ROW)])
    pair_lanes = lanes(y * 128, 128)

    def attend_rows(b, carry):
        here = rows(b * 256, 256)
        queries = f32(qkv[0, here, :]) * SCALE
        keys, values = qkv[1], qkv[2]
        allowed = tn(seg_q[:, lanes(b * 256, 256)], seg_k[...]) > 0.5
        outs = []
        for t in range(2):
            scores = nt(low(jnp.where(half_of_lane == t, queries, 0.0)), keys)
            scores = jnp.where(allowed, scores, MASKED)
            terms = jnp.exp(scores - jnp.max(scores, axis=-1, keepdims=True))
            weights = low(terms * (1.0 / jnp.sum(terms, axis=-1, keepdims=True)))
            p_low[t, here, :] = weights
            outs.append(nn(weights, values))
        out = jnp.where(half_of_lane == 0, outs[0], outs[1])
        att_f[here] = out
        att_low[here] = low(out)
        for t in range(2):
            there = 2 * b + t
            e7.send(att_low.at[rows(there * ROW, ROW)], att_all.at[mine, :, pair_lanes], there)

        return carry

    lax.fori_loop(0, GROUP // 256, attend_rows, 0)
    gather_output.stage4()
    for gather in gather_reduce:
        gather.stage4()
    for gather in gather_expand:
        gather.stage3()
    gather_output.finish()
    e7.wait(att_low.at[pl.ds(0, ROW)], att_all.at[mine, :, pair_lanes])

    branch = TeamSum(sums.branch)

    def branch_part(j):
        return nn(att_all[j], row_weight(output_s))

    branch.near(1, branch_part(diag))
    ref.far_a[...] = branch_part(far)
    branch.across(lambda part: ref.far_a[part])
    branch.near(0, branch_part(sib))
    ref.own_a[...] = branch_part(g)
    cot_handed = spread_on(cot_all, cot_copies[1])
    gather_expand[0].stage4()
    middle_ref = ref.middle
    middle_ref[...] = branch.total(ref.own_a[...]) + start_ref[...] + vector(OUTPUT_BIAS)

    class LineSum:
        def __init__(self, four, slot, yr, zr, za):
            self.four = four
            self.slot, self.yr, self.zr, self.za = slot, yr, zr, za
            self.at = reserve(6)

        def send(self, src, dst, device, i):
            remote(src, dst, device, self.at + i).start()

        def come(self, i):
            part = self.zr(0)
            remote(part, part, to_line(beside), self.at + i).wait_recv()

        def along_y(self):
            self.y_copies = Together(self.four)
            for i in range(4):
                self.y_copies.push(self.slot(2 * i + 1 - y), self.yr(i), to_line(beside))

        def add(self, place, came):
            block = self.slot(place)
            block[...] = low(f32(block[...]) + f32(came[...]))
            return block

        def sum_y(self):
            self.y_copies.wait_recv()

            def add(i, carry):
                self.add(2 * i + y, self.yr(i))
                return carry

            lax.fori_loop(0, 4, add, 0)

        def stage1(self):
            @pl.when(is_end)
            def _():
                for i, place in enumerate(far_places + [partner]):
                    self.send(self.slot(place), self.zr(i), to_line(partner), i)

        def stage2(self):
            @pl.when(is_middle)
            def _():
                for i, place in enumerate(far_places):
                    self.come(i)
                    block = self.add(place, self.zr(i))
                    self.send(block, self.za(i), to_line(facing), 3 + i)

        def stage3(self):
            @pl.when(is_middle)
            def _():
                for i in range(2):
                    self.come(3 + i)
                block = self.add(partner, self.za(1 - lax.rem(z, 2)))
                self.send(block, self.zr(0), to_line(partner), 5)

        def total(self, out):
            own = f32(self.slot(s)[...])

            @pl.when(is_middle)
            def _():
                self.come(2)
                total = own + f32(self.zr(2)[...]) + f32(self.za(lax.rem(z, 2))[...])
                out[...] = total.astype(out.dtype)

            @pl.when(is_end)
            def _():
                self.come(5)
                out[...] = (own + f32(self.zr(0)[...])).astype(out.dtype)

        def sent(self):
            part = self.zr(0)

            def gone(i):
                remote(part, part, to_line(beside), self.at + i).wait_send()

            @pl.when(is_middle)
            def _():
                for i in (3, 4, 5):
                    gone(i)

            @pl.when(is_end)
            def _():
                for i in range(3):
                    gone(i)

    class LineSumZ:
        def __init__(self, slot, zr, za, yr):
            self.slot, self.zr, self.za, self.yr = slot, zr, za, yr
            self.at = reserve(13)

        def both_y(self, place):
            return [place - y, place - y + 1]

        def send(self, src, dst, device, i):
            remote(src, dst, device, self.at + i).start()

        def come(self, i):
            part = self.zr(0)
            remote(part, part, to_line(beside), self.at + i).wait_recv()

        def add(self, place, came):
            block = self.slot(place)
            block[...] = low(f32(block[...]) + f32(came[...]))
            return block

        def stage1(self):
            @pl.when(is_end)
            def _():
                for i, place in enumerate(
                    self.both_y(far_places[0]) + self.both_y(far_places[1]) + self.both_y(partner)
                ):
                    self.send(self.slot(place), self.zr(i), to_line(partner), i)

        def stage2(self):
            @pl.when(is_middle)
            def _():
                for i, place in enumerate(self.both_y(far_places[0]) + self.both_y(far_places[1])):
                    self.come(i)
                    block = self.add(place, self.zr(i))
                    self.send(block, self.za(i), to_line(facing), 6 + i)

        def stage3(self):
            @pl.when(is_middle)
            def _():
                for i in range(4):
                    self.come(6 + i)
                for i, place in enumerate(self.both_y(partner)):
                    block = self.add(place, self.za(2 * (1 - lax.rem(z, 2)) + i))
                    self.send(block, self.zr(i), to_line(partner), 10 + i)
                for i, place in enumerate(self.both_y(s)):
                    self.come(4 + i)
                    self.add(place, self.zr(4 + i))
                    self.add(place, self.za(2 * lax.rem(z, 2) + i))

        def along_y(self):
            @pl.when(is_end)
            def _():
                for i, place in enumerate(self.both_y(s)):
                    self.come(10 + i)
                    self.add(place, self.zr(i))

            self.send(self.slot(beside), self.yr(0), to_line(beside), 12)

        def total(self, out):
            self.come(12)
            out[...] = f32(self.slot(s)[...]) + f32(self.yr(0)[...])

        def sent(self):
            part = self.zr(0)

            def gone(i):
                remote(part, part, to_line(beside), self.at + i).wait_send()

            gone(12)

            @pl.when(is_middle)
            def _():
                for i in (6, 7, 8, 9, 10, 11):
                    gone(i)

            @pl.when(is_end)
            def _():
                for i in range(6):
                    gone(i)

    def line_sum_of(gw, others, at=None, size=None):
        four = others[0]
        if at is None:
            return LineSum(four, whole(gw), *[whole(buf) for buf in others])
        if len(gw.shape) == 3:
            return LineSum(four, some_rows(gw, at, size), *[whole(buf) for buf in others])

        def part(buf):
            return lambda i: buf.at[i, :, :, pl.ds(at, size)]

        four = four.at[:, :, :, pl.ds(at, size)]
        return LineSum(four, some_lanes(gw, at, size), *[part(buf) for buf in others])

    output_sum = line_sum_of(ref.gw_output, [ref.yr_output, ref.zr_output, ref.za_output])
    merge_sum = line_sum_of(ref.gw_merge, [ref.yr_merge, ref.zr_merge, ref.za_merge])
    reduce_y = line_sum_of(
        ref.gw_reduce, [ref.yr_reduce, ref.zr_reduce, ref.za_reduce], 0, half_rows
    )
    reduce_z = LineSumZ(
        some_rows(ref.gw_reduce, half_rows, half_rows),
        whole(ref.zr_half),
        whole(ref.za_half),
        whole(ref.yr_half),
    )
    reduce_sums = [reduce_y, reduce_z]
    expand_sums = [
        line_sum_of(
            ref.gw_expand,
            [ref.yr_expand, ref.zr_expand, ref.za_expand],
            i * half_lanes,
            half_lanes,
        )
        for i in range(2)
    ]
    joint_sums = [
        line_sum_of(ref.gw_joint, [ref.yr_joint, ref.zr_joint, ref.za_joint], i * QC, QC)
        for i in range(3)
    ]

    second_all = ref.second_all
    second_all[g] = norm(
        middle_ref[...],
        ref.middle_hat,
        ref.middle_inv,
        vector(SECOND_GAIN),
        vector(SECOND_SHIFT),
    )
    second_copies = spread(second_all)
    for gather in [gather_expand[0]] + gather_reduce:
        gather.finish()
    cot_copies[0].wait_recv()
    wait_all(cot_handed)
    expand_s, reduce_s = ref.expand_s, ref.reduce_s
    active_all, gh_all = ref.active_all, ref.gh_all
    root = 0.7978845608028654

    def feed(j, k, acc_a, acc_b, half):
        def tile(i, carry):
            here = lanes(i * 256, 256)
            up = expand_s[:, :, :, here].reshape(D, 256)
            down = reduce_s[pl.ds(2 * i, 2)].reshape(256, D)
            hidden = nn(two(second_all, j, k), up) + shift_e[0:1, here]
            square = hidden * hidden
            bend = jnp.tanh(root * hidden * (1.0 + 0.044715 * square))
            active = low(0.5 * hidden * (1.0 + bend))
            slope = 0.5 * (1.0 + bend) + (0.5 * root) * hidden * (1.0 - bend * bend) * (
                1.0 + (3.0 * 0.044715) * square
            )
            grad = low(nt(two(cot_all, j, k), down) * slope)
            for n, block in enumerate((j, k)):
                active_all[block, :, here] = active[n * ROW : (n + 1) * ROW]
                gh_all[block, :, here] = grad[n * ROW : (n + 1) * ROW]
            for part, acc in ((nt(grad, up), acc_a), (nn(active, down), acc_b)):
                for n in range(2):
                    rows_of = part[n * ROW : (n + 1) * ROW]

                    @pl.when(i == 0)
                    def _():
                        acc[n][...] = rows_of

                    @pl.when(i > 0)
                    def _():
                        acc[n][...] += rows_of

            return carry

        lax.fori_loop(2 * half, 2 * half + 2, tile, 0)

    gw_expand = ref.gw_expand

    def expand_blocks(first, last, half):
        def block(i, carry):
            lhs = second_all[:, :, lanes(i * QC, QC)].reshape(TALL, QC)
            rhs = gh_all[:, :, half * half_lanes : (half + 1) * half_lanes].reshape(TALL, half_lanes)
            part = low(tn(lhs, rhs)).reshape(LINE, WD, half_lanes)
            gw_expand[i, :, :, half * half_lanes : (half + 1) * half_lanes] = part
            return carry

        lax.fori_loop(first, last, block, 0)

    second = TeamSum(sums.second)
    reduced = TeamSum(sums.reduced)
    own_a, own_b, far_a, far_b = ref.own_a, ref.own_b, ref.far_a, ref.far_b
    spare_a, spare_b = ref.grad_mid, ref.activations
    far_c, far_d = ref.g_reduce, ref.far_d
    near_blocks = (g, sib, (own_a, spare_a), (own_b, spare_b))
    far_blocks = (far, diag, (far_a, far_c), (far_b, far_d))
    second_copies[0].wait_recv()
    feed(*near_blocks, 0)
    second_handed = spread_on(second_all, second_copies[1])
    gather_expand[1].stage4()
    wait_all(second_handed)
    feed(*far_blocks, 0)
    expand_blocks(0, TEAM, 0)
    expand_sums[0].along_y()
    gather_expand[1].finish()
    feed(*near_blocks, 1)
    second.near(0, spare_a[...])
    reduced.ps[0] = low(spare_b[...])
    feed(*far_blocks, 1)
    second.near(1, far_c[...])
    reduced.ps[1] = low(far_d[...])
    second.across(lambda part: far_a[part])
    reduced.near(0)
    reduced.near(1)

    gw_reduce = ref.gw_reduce

    def reduce_block(j):
        lhs = active_all[:, :, lanes(j * ROW, ROW)].reshape(TALL, ROW)
        gw_reduce[j] = low(tn(lhs, tall(cot_all)))

    def reduce_beside(i, carry):
        reduce_block(2 * i + 1 - y)
        return carry

    def reduce_here(i, carry):
        reduce_block(2 * i + y)
        return carry

    lax.fori_loop(0, 4, reduce_beside, 0)
    reduce_y.along_y()
    lax.fori_loop(0, 4, reduce_here, 0)
    reduce_z.stage1()

    csum = ref.csum

    def note(i, value):
        csum[i : i + 1] = jnp.sum(value, axis=0, keepdims=True)

    grad_second = second.total(own_a[...])
    grad_mid = ref.grad_mid
    note(6, grad_second * ref.middle_hat[...])
    note(7, grad_second)
    grad_top = f32(cot_all[g])
    note(8, grad_top)
    grad_mid[...] = grad_top + norm_back_ref(
        grad_second, ref.middle_hat, ref.middle_inv, vector(SECOND_GAIN)
    )
    gb_all = ref.gb_all
    gb_all[g] = low(grad_mid[...])
    gb_copies = spread(gb_all)
    note(5, f32(gb_all[g]))
    g_send, go = ref.g_send, ref.go
    e12 = PairExchange(go.at[pl.ds(0, 7 * ROW)])

    def attended_back(i, j):
        part = low(nt(two(gb_all, i, j), row_weight(output_s)))
        for n, group in enumerate((i, j)):
            for t in range(2):
                g_send[group, t] = part[n * ROW : (n + 1) * ROW, t * 128 : (t + 1) * 128]
                e12.send(g_send.at[group, t], go.at[line_rows, :], pair_place(group, t))

    gb_copies[0].wait_recv()
    attended_back(g, sib)
    expand_blocks(0, 2, 1)
    gb_handed = spread_on(gb_all, gb_copies[1])
    wait_all(gb_handed)
    attended_back(far, diag)
    reduced.across(lambda part: far_b[part])
    expand_blocks(2, TEAM, 1)
    expand_sums[1].along_y()
    reduce_y.sum_y()
    reduce_y.stage1()
    gw_output = ref.gw_output
    gw_output[...] = low(tn(tall(att_all), tall(gb_all))).reshape(LINE, WD, D)
    e12.wait(g_send.at[0, 0], go.at[line_rows, :])
    output_sum.along_y()

    dq, d_all = ref.dq, ref.d_all
    dq[...] = jnp.zeros_like(dq)
    e13 = PairExchange(qkv.at[pl.ds(0, 2), pl.ds(0, 7 * ROW), :])
    products = f32(go[...]) * att_f[...]
    offsets = [
        jnp.sum(jnp.where(half_of_lane == t, products, 0.0), axis=-1, keepdims=True)
        for t in range(2)
    ]
    att_f[...] = jnp.where(half_of_lane == 0, offsets[0], offsets[1])
    pair_d = d_all.at[mine, pl.ds(1, 2), :, pair_lanes]

    def attend_back_keys(b, carry):
        here = rows(b * 256, 256)
        keys, values = qkv[1, here, :], qkv[2, here, :]
        queries, grad = f32(qkv[0]), f32(go[...])
        outs, grad_keys, grad_values = [], 0.0, 0.0
        for t in range(2):
            grad_t = low(jnp.where(half_of_lane == t, grad, 0.0))
            query_t = low(jnp.where(half_of_lane == t, queries, 0.0))
            weights = p_low[t, :, lanes(b * 256, 256)]
            offset = att_f[:, t * HDIM : t * HDIM + 1]
            slopes = low(low(f32(weights) * (nt(grad_t, values) - offset)) * SCALE)
            outs.append(nn(slopes, keys))
            grad_keys += tn(slopes, query_t)
            grad_values += tn(weights, grad_t)
        dq[...] += jnp.where(half_of_lane == 0, outs[0], outs[1])
        pair_send[pl.ds(2 * b, 2), 1] = low(grad_keys).reshape(2, ROW, 128)
        pair_send[pl.ds(2 * b, 2), 2] = low(grad_values).reshape(2, ROW, 128)
        for t in range(2):
            there = 2 * b + t
            e13.send(pair_send.at[there, pl.ds(1, 2)], pair_d, there)

        return carry

    lax.fori_loop(0, 2, attend_back_keys, 0)
    lax.fori_loop(2, GROUP // 256, attend_back_keys, 0)
    pair_send[:, 0] = low(dq[...]).reshape(LINE, ROW, 128)
    d_dst = d_all.at[mine, 0, :, pair_lanes]
    d_copies = to_whole_line(
        lambda place: pair_send.at[place, 0], d_dst, att_low.at[pl.ds(0, 7 * ROW)]
    )
    d_here = pltpu.make_async_copy(pair_send.at[s, 0], d_dst, recv.at[reserve(1)])
    d_here.start()
    d_here.wait()
    wait_all(d_copies)
    e13.wait(pair_send.at[0, pl.ds(1, 2)], pair_d)
    normed = TeamSum(sums.normed)

    def joint_back(j):
        total = None
        for kind in range(3):
            weight = joint_s[:, :, :, kind * QC : (kind + 1) * QC].reshape(D, QC)
            part = nt(d_all[j, kind], weight)
            total = part if total is None else total + part
        return total

    normed.near(1, joint_back(diag))
    far_a[...] = joint_back(far)
    normed.across(lambda part: far_a[part])
    for part in expand_sums:
        part.sum_y()
        part.stage1()
    reduce_z.stage2()
    normed.near(0, joint_back(sib))
    own_a[...] = joint_back(g)
    gw_joint = ref.gw_joint
    tsum = ref.tsum
    for kind in range(3):
        block = d_all[:, kind].reshape(TALL, QC)
        for i in range(TEAM):
            lhs = normed_all[:, :, i * QC : (i + 1) * QC].reshape(TALL, QC)
            part = low(tn(lhs, block)).reshape(LINE, WD, QC)
            gw_joint[i, :, :, kind * QC : (kind + 1) * QC] = part
        if kind != 1:
            row = 9 + kind // 2
            tsum[s, row : row + 1] = jnp.sum(f32(block), axis=0, keepdims=True)
    for part in joint_sums:
        part.along_y()
    hidden_sums = jnp.sum(f32(tall(gh_all)), axis=0, keepdims=True)
    for i in range(4):
        tsum[s, 11 + i : 12 + i] = hidden_sums[:, i * QC : (i + 1) * QC]
    tsum[s, 15:16] = jnp.zeros((1, QC), F32)

    grad_normed = normed.total(own_a[...])
    note(3, grad_normed * ref.start_hat[...])
    note(4, grad_normed)
    grad_start = grad_mid[...] + norm_back_ref(
        grad_normed, ref.start_hat, ref.start_inv, vector(FIRST_GAIN)
    )
    gm_all = ref.gm_all
    gm_all[g] = low(grad_start)
    gm_copies = spread(gm_all)
    note(0, f32(gm_all[g]))
    note(1, lead * grad_start)
    note(2, grad_start)
    csum[9:16] = jnp.zeros((7, D), F32)
    crecv = ref.crecv
    crecv[g] = csum[:, lanes(g * QC, QC)]
    c_copies = to_whole_team(
        lambda j: csum.at[:, lanes(j * QC, QC)], crecv.at[g], crecv.at[pl.ds(0, 3)]
    )
    ref.activations[...] = (
        reduced.total(own_b[...]) + middle_ref[...] + vector(REDUCE_BIAS)
    )
    deposit(ref.activations, results.activations)
    reduce_y.stage2()
    expand_sums[0].stage2()
    joint_sums[0].sum_y()
    joint_sums[0].stage1()
    gm_handed = spread_on(gm_all, gm_copies[1])
    gm_copies[0].wait_recv()
    wait_all(gm_handed)

    gw_merge = ref.gw_merge
    f_own = ref.f_own
    t_send = ref.t_send
    q_all = ref.q_all
    grad_heads = low(nt(tall(gm_all), row_weight(merge_s)))
    head_grad = ref.att_all
    head_grad[...] = grad_heads.reshape(TEAM, ROW, QC)
    q_all[s] = jnp.zeros((8, KP), F32)

    def choose_back(h):
        field = f32(tall(field_all))
        grad_h = low(jnp.where(head_of_lane == h, f32(tall(head_grad)), 0.0))
        value_back = nn(grad_h, pv[...].reshape(QC, KP))
        grad_chosen = split_dot(value_back * field, select[...])
        weights = chosen[h]
        shifted = grad_chosen - jnp.sum(weights * grad_chosen, axis=-1, keepdims=True)
        score_spread = nn(low(weights * shifted), select_t[...])
        spread_weights = nn(low(weights), select_t[...])
        pair = tall(head_grad)[:, (h // 2) * 128 : (h // 2 + 1) * 128]
        part = tn(pair, low(spread_weights * field))
        at_row = (h % 2) * HDIM
        t_send[2 * h : 2 * h + 2] = low(part[at_row : at_row + HDIM]).reshape(2, WD, KP)
        field_part = spread_weights * value_back + score_spread * probe[h : h + 1]
        field_part = field_part.reshape(TEAM, ROW, KP)
        if h == 0:
            f_own[...] = field_part
        else:
            f_own[...] += field_part
        q_all[s, h : h + 1] = jnp.sum(score_spread * field, axis=0, keepdims=True)

    for h in range(TEAM_HEADS):
        choose_back(h)
        if h == 0:
            reduce_z.stage3()
            joint_sums[1].sum_y()
            joint_sums[1].stage1()
        if h == 2:
            output_sum.sum_y()
            output_sum.stage1()
            expand_sums[1].stage2()
            reduce_y.stage3()
    t_recv = ref.t_recv
    t_copies = to_whole_line(
        lambda place: t_send.at[place], t_recv.at[s], t_recv.at[pl.ds(0, LINE - 1)]
    )
    t_recv[s] = t_send[s]
    q_copies = share_line(q_all)
    gw_merge[...] = low(tn(head_low[...], tall(gm_all))).reshape(LINE, WD, D)
    merge_sum.along_y()
    reduce_z.along_y()
    expand_sums[0].stage3()
    f_recv = ref.f_recv
    f_copies = Together(f_recv)
    for step in range(1, TEAM):
        j = lax.rem(g + step, TEAM)
        f_copies.push(f_own.at[j], f_recv.at[step - 1], to_team(j))
    position = jnp.zeros((ROW, QC), F32)
    for j in range(TEAM):
        position += f32(gm_all[j, :, lanes(g * QC, QC)])
    ref.g_position[...] = position
    deposit(ref.g_position, results.g_position)
    wait_all(c_copies)
    tsum[s, 0:9] = jnp.sum(crecv[...], axis=0)[0:9]

    joint_sums[0].stage2()
    joint_sums[2].sum_y()
    joint_sums[2].stage1()
    joint_sums[1].stage2()
    expand_sums[1].stage3()
    output_sum.stage2()
    joint_sums[2].stage2()
    merge_sum.sum_y()
    merge_sum.stage1()
    wait_all(t_copies)
    head_all, score_all = ref.head_all, ref.score_all
    head_all[g, s] = low(jnp.sum(f32(t_recv[...]), axis=0))
    h_here = head_all.at[g, s]
    h_copies = to_whole_line(lambda place: h_here, h_here, head_all.at[0, pl.ds(0, LINE - 1)])
    joint_sums[0].stage3()
    joint_sums[1].stage3()
    output_sum.stage3()
    merge_sum.stage2()

    xs_joint, xs_expand = ref.xs_joint, ref.xs_expand
    xr_joint, xr_expand = ref.xr_joint, ref.xr_expand
    x_copies = []

    def to_owners(line_sum, xs, xr, at, size):
        here = pl.ds(at, size)
        line_sum.total(xs.at[:, :, here])
        x_copies.extend(
            to_whole_team(
                lambda j: xs.at[j, :, here], xr.at[g, :, here], xr.at[pl.ds(0, 3), :, here]
            )
        )
        xr[g, :, here] = xs[g, :, here]

    to_owners(expand_sums[0], xs_expand, xr_expand, 0, half_lanes)
    joint_sums[2].stage3()
    to_owners(joint_sums[0], xs_joint, xr_joint, 0, QC)
    wait_all(h_copies)
    h_spread = spread(head_all)
    s_copies = share_line(tsum)
    merge_sum.stage3()
    wait_all(q_copies)
    score_all[g] = jnp.sum(q_all[...], axis=0)
    score_here = score_all.at[g]
    score_copies = to_whole_team(lambda j: score_here, score_here, score_all.at[pl.ds(0, 3)])
    to_owners(expand_sums[1], xs_expand, xr_expand, half_lanes, half_lanes)
    to_owners(joint_sums[1], xs_joint, xr_joint, QC, QC)
    h_handed = spread_on(head_all, h_spread[1])
    to_owners(joint_sums[2], xs_joint, xr_joint, 2 * QC, QC)
    for i in range(2):
        reduce_sums[i].total(ref.g_reduce.at[pl.ds(i * half_rows, half_rows)])
    deposit(ref.g_reduce, results.g_reduce)
    output_sum.total(ref.g_output)
    deposit(ref.g_output, results.g_output)
    f_copies.wait_recv()
    ref.field_grad[...] = (f_own[g] + f_recv[0] + f_recv[1] + f_recv[2]).T[0:VP]
    deposit(ref.field_grad, results.field_grad)
    wait_all(s_copies)
    ref.sums[...] = jnp.sum(tsum[...], axis=0)
    merge_sum.total(ref.g_merge)
    deposit(ref.g_merge, results.g_merge)
    wait_all(x_copies)
    for j in range(TEAM):
        ref.g_expand[:, j * D : (j + 1) * D] = f32(xr_expand[j])
        for kind in range(3):
            at_lane = kind * D + j * QC
            ref.g_joint[:, at_lane : at_lane + QC] = f32(
                xr_joint[j, :, kind * QC : (kind + 1) * QC]
            )
    deposit(ref.g_expand, results.g_expand)
    deposit(ref.g_joint, results.g_joint)
    wait_all(score_copies)
    score_rows = ref.score_rows
    for j in range(TEAM):
        score_rows[TEAM_HEADS * j : TEAM_HEADS * (j + 1)] = score_all[j, 0:TEAM_HEADS]

    def exact(a, b, ca, cb):
        return lax.dot_general(
            a,
            b,
            (((ca,), (cb,)), ((), ())),
            precision=lax.Precision.HIGHEST,
            preferred_element_type=F32,
        )

    scores = score_rows[...]
    query_row = vector(QUERY)
    head_of = lax.broadcasted_iota(jnp.int32, (16, D), 1) // HDIM
    head_rows = (head_of == lax.broadcasted_iota(jnp.int32, (16, D), 0)).astype(F32)
    probe_own = f32(
        low(exact(f32(ref.key_w[...]) * query_row, head_rows, 1, 1) * SCALE)
    )
    grad_probe = exact(f32(pe[...]), scores, 1, 1)
    ref.g_key[...] = exact(grad_probe, head_rows, 1, 0) * (query_row * SCALE)
    deposit(ref.g_key, results.g_key)
    small = ref.small
    picks = (
        lax.broadcasted_iota(jnp.int32, (QC, 128), 0)
        == lax.broadcasted_iota(jnp.int32, (QC, 128), 1) + s * WD
    ) & (lax.broadcasted_iota(jnp.int32, (QC, 128), 1) < WD)
    small[16:24] = jnp.zeros((8, 128), F32)
    small[0:SUM_ROWS] = exact(ref.sums[...], picks.astype(F32), 1, 0)
    hidden_row = jnp.zeros((1, QC), F32)
    score_row = jnp.zeros((1, KP), F32)
    own_scores = score_all[g]
    for i in range(4):
        hidden_row = jnp.where(s // 2 == i, ref.sums[11 + i : 12 + i], hidden_row)
        score_row = jnp.where(s // 2 == i, own_scores[i : i + 1], score_row)
    hidden_row = jnp.where(s % 2 == 0, hidden_row[:, 0:128], hidden_row[:, 128:256])
    query_grad = exact(jnp.broadcast_to(score_row, (8, KP)), ref.key_own[...], 1, 1) * SCALE
    small[24:32] = jnp.zeros((8, 128), F32)
    small[24:25] = hidden_row
    small[25:26, 0:WD] = query_grad[0:1]
    deposit(small, results.small)
    h_spread[0].wait_recv()
    wait_all(h_handed)
    heads = head_all[...].reshape(D, KP)
    ref.g_value[...] = nt(pe[...], heads)
    deposit(ref.g_value, results.g_value)
    grad_table = nn(ref.value_w[...], heads) + exact(probe_own, scores, 1, 0)
    ref.g_patch[...] = grad_table[:, 0:VP]
    ref.g_embed[...] = grad_table[:, VP : VP + VARS]
    deposit(ref.g_patch, results.g_patch)
    deposit(ref.g_embed, results.g_embed)
    for copy in begun + begun_together:
        copy.wait_send()
    for gather in [gather_merge, gather_output] + gather_reduce + gather_joint + gather_expand:
        gather.sent()
    for line_sum in [output_sum, merge_sum] + reduce_sums + joint_sums + expand_sums:
        line_sum.sent()
    for copy in deposits:
        copy.wait()


def fused(operands):
    scratch = list(SCRATCH.values()) + list(OUTPUTS.values())
    for shape in TEAM_SUMS.values():
        scratch += team_sum_buffers(shape)
    return pl.pallas_call(
        fused_kernel,
        out_shape=[jax.ShapeDtypeStruct(*shape) for shape in OUTPUTS.values()],
        in_specs=[pl.BlockSpec(memory_space=space) for space in INPUTS.values()],
        out_specs=[pl.BlockSpec(memory_space=pl.ANY)] * len(OUTPUTS),
        scratch_shapes=[pltpu.VMEM(*shape) for shape in scratch]
        + [pltpu.SemaphoreType.DMA((SEMAPHORES,))] * 2,
        compiler_params=pltpu.CompilerParams(
            collective_id=1, has_side_effects=True, vmem_limit_bytes=64 << 20
        ),
    )(*operands)


VECTOR_ROWS = (25, 0, 1, 2, 3, 4, 5, 6, 7, 8)


def hand_out_kernel(*refs):
    n, m = len(OUTPUTS), len(VECTOR_ROWS)
    arrays = refs[:n]
    results = refs[n : 2 * n - 1]
    vectors = refs[2 * n - 1 : 2 * n - 1 + m]
    joint, hidden = refs[2 * n - 1 + m : 2 * n + 1 + m]
    held = refs[2 * n + 1 + m : 3 * n + 1 + m]
    narrow, both, came, left = refs[3 * n + 1 + m :]
    fetches = [pltpu.make_async_copy(arrays[i], held[i], came.at[i]) for i in range(n)]
    for copy in fetches:
        copy.start()
    small = held[n - 1]
    fetches[n - 1].wait()
    narrow[...] = small[:, 0:WD]
    both[...] = small[9:11, 0:WD]
    stores = [
        pltpu.make_async_copy(narrow.at[row], vectors[i], left.at[n + i])
        for i, row in enumerate(VECTOR_ROWS)
    ]
    stores.append(pltpu.make_async_copy(both, joint, left.at[n + m]))
    stores.append(pltpu.make_async_copy(small.at[24], hidden, left.at[n + m + 1]))
    for copy in stores:
        copy.start()
    for i in range(n - 1):
        fetches[i].wait()
        copy = pltpu.make_async_copy(held[i], results[i], left.at[i])
        copy.start()
        stores.append(copy)
    for copy in stores:
        copy.wait()


def hand_out(arrays):
    n, m = len(arrays), len(VECTOR_ROWS)
    shapes = [jax.ShapeDtypeStruct(a.shape, a.dtype) for a in arrays[:-1]]
    shapes += [jax.ShapeDtypeStruct((WD,), F32)] * m
    shapes += [jax.ShapeDtypeStruct((2, WD), F32), jax.ShapeDtypeStruct((ROW,), F32)]
    return pl.pallas_call(
        hand_out_kernel,
        out_shape=shapes,
        in_specs=[pl.BlockSpec(memory_space=pl.ANY)] * n,
        out_specs=[pl.BlockSpec(memory_space=pl.ANY)] * len(shapes),
        scratch_shapes=[pltpu.VMEM(a.shape, a.dtype) for a in arrays]
        + [pltpu.VMEM((32, WD), F32), pltpu.VMEM((2, WD), F32)]
        + [pltpu.SemaphoreType.DMA((n,)), pltpu.SemaphoreType.DMA((n + m + 2,))],
        compiler_params=pltpu.CompilerParams(vmem_limit_bytes=64 << 20),
    )(*arrays)


def shards_fused(
    fields,
    patch_weight,
    variable_embed,
    query_vector,
    key_weight,
    value_weight,
    merge_weight,
    merge_bias,
    position_table,
    lead_weight,
    lead_bias,
    first_gain,
    first_shift,
    joint_weight,
    joint_bias,
    output_weight,
    output_bias,
    second_gain,
    second_shift,
    expand_weight,
    expand_bias,
    reduce_weight,
    reduce_bias,
    segment_ids,
    live_rows,
    lead_steps,
    cotangent,
):
    pack = jnp.concatenate(
        [
            query_vector,
            merge_bias,
            lead_weight,
            lead_bias,
            first_gain,
            first_shift,
            output_bias,
            second_gain,
            second_shift,
            reduce_bias,
            jnp.zeros((2 * WD,), BF16),
            expand_bias,
            jnp.zeros((12 * 128,), BF16),
        ]
    ).reshape(16, 128)
    whole = fused(
        (
            fields.T,
            patch_weight.T,
            variable_embed.T,
            key_weight,
            value_weight,
            pack,
            joint_bias,
            segment_ids.reshape(1, ROW),
            live_rows.reshape(1, ROW),
            lead_steps,
            cotangent,
            position_table,
            joint_weight,
            expand_weight,
            merge_weight,
            output_weight,
            reduce_weight,
        )
    )
    (
        activations,
        field_grad,
        g_patch,
        g_embed,
        g_key,
        g_value,
        g_merge,
        g_position,
        g_joint,
        g_output,
        g_expand,
        g_reduce,
        g_query,
        g_merge_b,
        g_lead,
        g_lead_b,
        g_first_gain,
        g_first_shift,
        g_output_b,
        g_second_gain,
        g_second_shift,
        g_reduce_b,
        g_joint_b,
        g_expand_b,
    ) = hand_out(whole)
    return (
        activations,
        field_grad.T,
        g_patch.T,
        g_embed.T,
        g_query,
        g_key,
        g_value,
        g_merge,
        g_merge_b,
        g_position,
        g_lead,
        g_lead_b,
        g_first_gain,
        g_first_shift,
        g_joint,
        g_joint_b,
        g_output,
        g_output_b,
        g_second_gain,
        g_second_shift,
        g_expand,
        g_expand_b,
        g_reduce,
        g_reduce_b,
    )


def solution(mesh):
    by_row = P(ROWS, None)
    by_column = P(None, ROWS)
    vector = P(ROWS)
    in_specs = (
        by_row,
        by_column,
        by_column,
        vector,
        by_row,
        by_row,
        by_row,
        vector,
        P("seq", "grp"),
        vector,
        vector,
        vector,
        vector,
        by_row,
        by_column,
        by_row,
        vector,
        vector,
        vector,
        by_row,
        vector,
        by_row,
        vector,
        vector,
        vector,
        P("grp", None),
        by_row,
    )
    out_specs = (
        by_row,
        by_row,
        by_column,
        by_column,
        vector,
        by_row,
        by_row,
        by_row,
        vector,
        P("seq", "grp"),
        vector,
        vector,
        vector,
        vector,
        by_row,
        by_column,
        by_row,
        vector,
        vector,
        vector,
        by_row,
        vector,
        by_row,
        vector,
    )
    G, S = mesh.shape["grp"], mesh.shape["seq"]

    def body(*args):
        rows_here, weight_rows = args[0].shape[0], args[5].shape[0]
        if (G, S, rows_here, weight_rows) == (TEAM, LINE, ROW, WD):
            return shards_fused(*args)
        return shards(G, S, *args)

    return jax.shard_map(body, mesh=mesh, in_specs=in_specs, out_specs=out_specs, check_vma=False)
```

profile of v0, /device:TPU:0, one launch (start us, length us, event | category | flops | bytes accessed | tf_op | source)
XLA Modules:
  0.0 239.0 jit_solution(13559334155663277712)
XLA Ops:
  0.7 0.0 copy-start.9
  0.7 0.0 copy-start
  0.7 0.0 copy-start.1
  0.7 0.0 copy-start.2
  0.7 0.0 copy-start.3
  0.7 0.0 copy-start.4
  0.7 0.0 copy-start.5
  0.8 0.0 copy-start.6
  0.8 0.0 copy-start.7
  0.8 0.0 copy-start.8
  0.8 0.5 copy-done.9
  1.3 0.0 copy-done.10
  1.3 0.0 copy-done
  1.3 0.0 copy-done.1
  1.4 0.0 copy-done.2
  1.4 0.0 copy-done.3
  1.4 0.0 copy-done.4
  1.4 0.0 copy-done.5
  1.4 0.0 copy-done.6
  1.4 0.0 copy-done.7
  1.5 0.0 copy-done.8
  1.5 0.7 concatenate.3
  2.2 233.1 %shard_map.442 = (f32[128,1024]{1,0:T(8,128)}, f32[192,128]{1,0:T(8,128)}, f32[32,192]{1,0:T(8,128)}, f32[32,48]{1,0:T(8,128)}, f32[32,1024]{1,0:T(8,128)}, /*in...) custom-call(bf16[192,128]{1,0:T(8,128)(2,1)} %bitcast.9, ...), custom_call_target="tpu_custom_call" | custom-call | tf_op jit(solution)/shard_map/pallas_call | solution.py:2006
  235.3 3.5 %shard_map.443 = (f32[128,1024]{1,0:T(8,128)}, f32[192,128]{1,0:T(8,128)}, f32[32,192]{1,0:T(8,128)}, f32[32,48]{1,0:T(8,128)}, f32[32,1024]{1,0:T(8,128)}, /*in...) custom-call(f32[128,1024]{1,0:T(8,128)} %get-tuple-element.61.refs_0, ...), custom_call_target="tpu_custom_call" | custom-call | tf_op jit(solution)/shard_map/pallas_call | solution.py:2059
  (3 shorter events, 0.0 us)
Async XLA Ops:
  0.7 0.7 copy-start.9
  0.7 0.7 copy-start.10
  0.7 0.7 copy-start
  0.7 0.7 copy-start.1
  0.7 0.7 copy-start.2
  0.7 0.7 copy-start.3
  0.7 0.7 copy-start.4
  0.7 0.7 copy-start.5
  0.8 0.7 copy-start.6
  0.8 0.7 copy-start.7
  0.8 0.7 copy-start.8
where the time goes:
time: 239 us
  Pallas kernels  237 us (99%)
    pallas_call x1, Pallas kernels, fused(): pl.pallas_call(fused_kernel, out_shape=[jax.ShapeDtypeStruct(*shape) for...  233 us

commit v1 on v0

--- a/solution.py
+++ b/solution.py
@@ -703,7 +703,8 @@
     return (near, near, one, one)
 
 
-SEMAPHORES = 252
+SEMAPHORES = 223
+HERE = 29
 
 
 def nn(a, b):
@@ -733,7 +734,7 @@
     rest = refs[:n_in] + refs[n_in + n_out :]
     ref = types.SimpleNamespace(**dict(zip(names, rest)))
     rest = rest[len(names) :]
-    send, recv = rest[-2:]
+    send, recv, here_sems = rest[-3:]
     sums = dict(zip(TEAM_SUMS, [rest[4 * i : 4 * i + 4] for i in range(len(TEAM_SUMS))]))
     sums = types.SimpleNamespace(**sums)
     g = lax.axis_index("grp")
@@ -767,6 +768,13 @@
         assert used[0] <= SEMAPHORES
         return at
 
+    used_here = [0]
+
+    def reserve_here():
+        used_here[0] += 1
+        assert used_here[0] <= HERE
+        return used_here[0] - 1
+
     def remote(src, dst, device, at):
         return pltpu.make_async_remote_copy(
             src_ref=src,
@@ -858,7 +866,7 @@
     deposits = []
 
     def deposit(src, dst):
-        copy = pltpu.make_async_copy(src, dst, recv.at[reserve(1)])
+        copy = pltpu.make_async_copy(src, dst, here_sems.at[reserve_here()])
         copy.start()
         deposits.append(copy)
 
@@ -947,7 +955,7 @@
 
     class PairExchange:
         def __init__(self, bulk):
-            self.group, self.own = Together(bulk, waits_itself=True), reserve(1)
+            self.group, self.own = Together(bulk, waits_itself=True), reserve_here()
 
         def send(self, src, dst, there):
             @pl.when(there != s)
@@ -956,10 +964,10 @@
 
             @pl.when(there == s)
             def _():
-                pltpu.make_async_copy(src, dst, recv.at[self.own]).start()
+                pltpu.make_async_copy(src, dst, here_sems.at[self.own]).start()
 
         def wait(self, src, dst):
-            pltpu.make_async_copy(src, dst, recv.at[self.own]).wait()
+            pltpu.make_async_copy(src, dst, here_sems.at[self.own]).wait()
             self.group.wait_recv()
             self.group.wait_send()
 
@@ -1017,7 +1025,7 @@
     local = []
 
     def keep(src, dst):
-        copy = pltpu.make_async_copy(src, dst, recv.at[reserve(1)])
+        copy = pltpu.make_async_copy(src, dst, here_sems.at[reserve_here()])
         copy.start()
         local.append(copy)
 
@@ -1730,7 +1738,7 @@
     d_copies = to_whole_line(
         lambda place: pair_send.at[place, 0], d_dst, att_low.at[pl.ds(0, 7 * ROW)]
     )
-    d_here = pltpu.make_async_copy(pair_send.at[s, 0], d_dst, recv.at[reserve(1)])
+    d_here = pltpu.make_async_copy(pair_send.at[s, 0], d_dst, here_sems.at[reserve_here()])
     d_here.start()
     d_here.wait()
     wait_all(d_copies)
@@ -2009,7 +2017,8 @@
         in_specs=[pl.BlockSpec(memory_space=space) for space in INPUTS.values()],
         out_specs=[pl.BlockSpec(memory_space=pl.ANY)] * len(OUTPUTS),
         scratch_shapes=[pltpu.VMEM(*shape) for shape in scratch]
-        + [pltpu.SemaphoreType.DMA((SEMAPHORES,))] * 2,
+        + [pltpu.SemaphoreType.DMA((SEMAPHORES,))] * 2
+        + [pltpu.SemaphoreType.DMA((HERE,))],
         compiler_params=pltpu.CompilerParams(
             collective_id=1, has_side_effects=True, vmem_limit_bytes=64 << 20
         ),
@@ -2030,23 +2039,24 @@
     fetches = [pltpu.make_async_copy(arrays[i], held[i], came.at[i]) for i in range(n)]
     for copy in fetches:
         copy.start()
+    stores = []
+    for i in range(n - 1):
+        fetches[i].wait()
+        stores.append(pltpu.make_async_copy(held[i], results[i], left.at[i]))
+        stores[-1].start()
     small = held[n - 1]
     fetches[n - 1].wait()
     narrow[...] = small[:, 0:WD]
     both[...] = small[9:11, 0:WD]
-    stores = [
+    last = [
         pltpu.make_async_copy(narrow.at[row], vectors[i], left.at[n + i])
         for i, row in enumerate(VECTOR_ROWS)
     ]
-    stores.append(pltpu.make_async_copy(both, joint, left.at[n + m]))
-    stores.append(pltpu.make_async_copy(small.at[24], hidden, left.at[n + m + 1]))
-    for copy in stores:
+    last.append(pltpu.make_async_copy(both, joint, left.at[n + m]))
+    last.append(pltpu.make_async_copy(small.at[24], hidden, left.at[n + m + 1]))
+    for copy in last:
         copy.start()
-    for i in range(n - 1):
-        fetches[i].wait()
-        copy = pltpu.make_async_copy(held[i], results[i], left.at[i])
-        copy.start()
-        stores.append(copy)
+    stores += last
     for copy in stores:
         copy.wait()
 

time: 239 us -> 238 us (level)
  no operation moved by 1% of the time
where the time goes in v1:
time: 238 us
  Pallas kernels  236 us (99%)
    pallas_call x1, Pallas kernels, fused(): pl.pallas_call(fused_kernel, out_shape=[jax.ShapeDtypeStruct(*shape) for...  233 us

profile of v1, /device:TPU:0, one launch (start us, length us, event | category | flops | bytes accessed | tf_op | source)
XLA Modules:
  0.0 238.2 jit_solution(7216650579167388257)
XLA Ops:
  0.7 0.0 copy-start.9
  0.7 0.0 copy-start
  0.7 0.0 copy-start.1
  0.7 0.0 copy-start.2
  0.7 0.0 copy-start.3
  0.7 0.0 copy-start.4
  0.7 0.0 copy-start.5
  0.8 0.0 copy-start.6
  0.8 0.0 copy-start.7
  0.8 0.0 copy-start.8
  0.8 0.5 copy-done.9
  1.3 0.0 copy-done.10
  1.3 0.0 copy-done
  1.3 0.0 copy-done.1
  1.4 0.0 copy-done.2
  1.4 0.0 copy-done.3
  1.4 0.0 copy-done.4
  1.4 0.0 copy-done.5
  1.4 0.0 copy-done.6
  1.4 0.0 copy-done.7
  1.5 0.0 copy-done.8
  1.5 0.7 concatenate.3
  2.2 232.9 %shard_map.442 = (f32[128,1024]{1,0:T(8,128)}, f32[192,128]{1,0:T(8,128)}, f32[32,192]{1,0:T(8,128)}, f32[32,48]{1,0:T(8,128)}, f32[32,1024]{1,0:T(8,128)}, /*in...) custom-call(bf16[192,128]{1,0:T(8,128)(2,1)} %bitcast.9, ...), custom_call_target="tpu_custom_call" | custom-call | tf_op jit(solution)/shard_map/pallas_call | solution.py:2014
  235.0 3.0 %shard_map.443 = (f32[128,1024]{1,0:T(8,128)}, f32[192,128]{1,0:T(8,128)}, f32[32,192]{1,0:T(8,128)}, f32[32,48]{1,0:T(8,128)}, f32[32,1024]{1,0:T(8,128)}, /*in...) custom-call(f32[128,1024]{1,0:T(8,128)} %get-tuple-element.61.refs_0, ...), custom_call_target="tpu_custom_call" | custom-call | tf_op jit(solution)/shard_map/pallas_call | solution.py:2069
  (3 shorter events, 0.0 us)
Async XLA Ops:
  0.7 0.7 copy-start.9
  0.7 0.7 copy-start.10
  0.7 0.7 copy-start
  0.7 0.7 copy-start.1
  0.7 0.7 copy-start.2
  0.7 0.7 copy-start.3
  0.7 0.7 copy-start.4
  0.7 0.7 copy-start.5
  0.8 0.7 copy-start.6
  0.8 0.7 copy-start.7
  0.8 0.7 copy-start.8
